TPU v7x, 32 devices: a whole 2x2x4 slice. The times are simulated.
32 devices in a mesh: member: 2 (over x), col: 16 (over z, y, core).
Axes of the slice: x: 2, y: 2, z: 4, core: 2. Of those that a mesh axis runs over, the one named last changes fastest.
Arguments:
- air_prognostic_variables: float32 [3, 72, 65536], P(None, None, ('member', 'col')), parts along dimension 2, may hold values from -6 to 6
- air_observed_warmth: float32 [65536], P(('member', 'col')), parts along dimension 0, may hold values from -6 to 6
- air_adjacency_list: int32 [4, 32768], P(None, 'col'), may hold values from 0 to 2303, as said below
- air_diffusivity_profile: float32 [72, 72], replicated, may hold values from 0 to 0.0075
- marine_prognostic_variables: float32 [3, 80, 32768], P(None, None, ('member', 'col')), parts along dimension 2, may hold values from -6 to 6
- sealevel_elevation: float32 [32768], P(('member', 'col')), parts along dimension 0, may hold values from -6 to 6
- marine_adjacency_lists: int32 [6, 16384], P(None, 'col'), may hold values from 0 to 1279, as said below
- marine_face_factors: float32 [6, 16384], P(None, 'col'), may hold values from 0.02 to 0.14
- marine_indicator: int32 [16384], P('col'), may hold values 0 or 1
- marine_diffusivity_profile: float32 [80, 80], replicated, may hold values from 0 to 0.0075
- interpolation_donor_group: int32 [128, 4], replicated, may hold values from 0 to 255, as said below
- interpolation_factor_array: float32 [128, 4, 128, 128], P('col'), may hold values from 0.0005 to 0.005
Outputs:
- atm_out: float32 [3, 72, 65536], P(None, None, ('member', 'col')), parts along dimension 2
- ocn_out: float32 [3, 80, 32768], P(None, None, ('member', 'col')), parts along dimension 2
- ssh_out: float32 [32768], P(('member', 'col')), parts along dimension 0
- skin_upon_air_grid: float32 [3, 65536], P(None, ('member', 'col')), parts along dimension 1
There are 2 independent parts, one for each index of `member`. A program takes and returns all parts, laid end to end along the dimension named above; an argument that names none is the same for every part. Nothing has to cross between parts.
Inputs may be any that keep to these rules, and one draw needn't show every extreme that they name: `air_adjacency_list`: entry [k, c] names the neighbour g_a(k, c) of the steps; every neighbour lies within 128 columns of c. `marine_adjacency_lists`: entry [k, c] names the neighbour g_o(k, c) of the steps; every neighbour lies within 128 cells of c. `interpolation_donor_group`: ocean block B lies on col index B // 8, atmosphere block A on index A // 16. Of the 32 references of the ocean blocks of one index, exactly 16 name atmosphere blocks of the same index; each other one names a block of the index one below or one above, wrapping around.
All inputs are finite; a program needn't handle non-finite values. No bound on the sum of `marine_indicator` on one device may be relied on, other than what follows from the above.
Results may differ from a plain program's by a relative error of at most 0.0001.
Values sent between devices are 32-bit elements; how exact they have to be, the bound alone decides.
A program may use at most 64 MiB of HBM per device.

v0:
```python
import jax
import jax.numpy as jnp
from jax import lax
from jax.sharding import PartitionSpec as P

RIM_A = 128
SUB_A = 4
RIM_O = 128
BT_SUB = 10
BC_SUB = 2
NFLUX = 4
NBACK = 4
REFS = 4
BLOCK = 128


highest = lax.Precision.HIGHEST


def with_halo(array, sides, width):
    for axis, dim in sides:
        size, length = (lax.axis_size(axis), array.shape[dim])
        up = [(i, (i + 1) % size) for i in range(size)]
        down = [(j, i) for i, j in up]
        last = lax.slice_in_dim(array, length - width, length, axis=dim)
        initial = lax.slice_in_dim(array, 0, width, axis=dim)
        before = lax.ppermute(last, axis, up)
        after = lax.ppermute(initial, axis, down)
        array = jnp.concatenate([before, array, after], axis=dim)
    return array


def skin_interface_transfers(lowermost_layer, prior_skin_warmth):
    return jnp.stack(
        [
            0.5 * (lowermost_layer[0] - prior_skin_warmth),
            0.3 * lowermost_layer[1] * lowermost_layer[2],
            0.5 * lowermost_layer[1],
            0.5 * lowermost_layer[2],
        ]
    )


def link_operator(links, weights, reach):
    count, cells = links.shape
    blocks = cells // BLOCK
    span = BLOCK + 2 * reach
    starts = (jnp.arange(blocks, dtype=jnp.int32) * BLOCK)[None, :, None]
    local = links.reshape(count, blocks, BLOCK) - starts
    window_ids = jnp.arange(span, dtype=jnp.int32)[None, :, None]
    operator = jnp.zeros((blocks, span, BLOCK), jnp.float32)
    for neighbour in range(count):
        hits = local[neighbour][:, None, :] == window_ids
        factor = weights[neighbour].reshape(blocks, 1, BLOCK)
        operator = operator + jnp.where(hits, factor, 0.0)
    return operator


def apply_operator(extended, operator):
    blocks, span, width = operator.shape
    lead = extended.shape[:-1]
    length = extended.shape[-1]
    flat = extended.reshape((-1, length // BLOCK, BLOCK))
    windows = jnp.concatenate(
        [flat[:, part : part + blocks] for part in range(span // BLOCK)], axis=-1
    )
    result = jnp.einsum("rbw,bwo->rbo", windows, operator, precision=highest)
    return result.reshape(lead + (blocks * BLOCK,))


def atm_update(extended, center, operator, count, mixing):
    totals = apply_operator(extended, operator) - count * center
    blended = center + 0.22 * totals
    return 0.6 * blended + jnp.einsum("lm,fmc->flc", mixing, blended, precision=highest)


def ocean_spread(extended, center, operator, weight_total):
    return apply_operator(extended, operator) - weight_total * center


def baroclinic_column(
    column_state, ocean_mask, ocn_operator, weight_total, marine_diffusivity_profile, forcing
):
    extended = with_halo(column_state, (("col", 2),), RIM_O)
    blended = column_state + ocean_spread(extended, column_state, ocn_operator, weight_total)
    column_state = ocean_mask * (
        0.6 * blended
        + jnp.einsum("lm,fmc->flc", marine_diffusivity_profile, blended, precision=highest)
    )
    return column_state.at[:, 0, :].add(forcing)


def body(
    air_prognostic_variables,
    air_observed_warmth,
    air_adjacency_list,
    air_diffusivity_profile,
    marine_prognostic_variables,
    sealevel_elevation,
    marine_adjacency_lists,
    marine_face_factors,
    marine_indicator,
    marine_diffusivity_profile,
    interpolation_donor_group,
    interpolation_factor_array,
):
    devices = lax.axis_size("col")
    rank_here = lax.axis_index("col")
    atm_cells = air_prognostic_variables.shape[2]
    ocn_cells = marine_prognostic_variables.shape[2]
    atm_blocks = atm_cells // BLOCK
    ocn_blocks = ocn_cells // BLOCK
    atm_count = air_adjacency_list.shape[0]
    lowermost_layer = air_prognostic_variables[:, -1, :]
    interface_transfers = skin_interface_transfers(lowermost_layer, air_observed_warmth)
    atm_now = air_prognostic_variables
    unit_weights = jnp.ones(air_adjacency_list.shape, jnp.float32)
    atm_operator = link_operator(air_adjacency_list, unit_weights, RIM_A)
    for substep in range(SUB_A):
        extended = with_halo(atm_now, (("col", 2),), RIM_A)
        atm_now = atm_update(extended, atm_now, atm_operator, atm_count, air_diffusivity_profile)
    ref_ids = lax.dynamic_slice_in_dim(
        interpolation_donor_group, rank_here * ocn_blocks, ocn_blocks, 0
    ).reshape(-1)
    source_rank = ref_ids // atm_blocks
    local_block = ref_ids % atm_blocks
    offset = (source_rank - rank_here) % devices
    arrived = with_halo(interface_transfers, (("col", 1),), atm_cells)
    candidates = arrived.reshape(NFLUX, 3 * atm_blocks, BLOCK)
    position = jnp.where(
        offset == 0,
        atm_blocks + local_block,
        jnp.where(offset == 1, 2 * atm_blocks + local_block, local_block),
    )
    pick_table = (position[:, None] == jnp.arange(3 * atm_blocks, dtype=jnp.int32)[None, :]).astype(
        jnp.float32
    )
    picked = jnp.einsum("mt,ftc->fmc", pick_table, candidates, precision=highest).reshape(
        NFLUX, ocn_blocks, REFS, BLOCK
    )
    ocean_flux = jnp.einsum(
        "brao,fbra->fbo", interpolation_factor_array, picked, precision=highest
    ).reshape(NFLUX, ocn_cells)
    ocean_mask = marine_indicator.astype(jnp.float32)
    column_state = marine_prognostic_variables * ocean_mask
    surface_height = sealevel_elevation * ocean_mask
    freshwater = 0.1 * ocean_flux[1]
    forcing = 0.2 * jnp.stack([ocean_flux[0], ocean_flux[2], ocean_flux[3]]) * ocean_mask
    ocn_operator = link_operator(marine_adjacency_lists, marine_face_factors, RIM_O)
    weight_total = jnp.sum(marine_face_factors, axis=0)

    def barotropic(counter, height):
        extended = with_halo(height, (("col", 0),), RIM_O)
        return ocean_mask * (
            height + ocean_spread(extended, height, ocn_operator, weight_total) + freshwater
        )

    for baroclinic in range(BC_SUB):
        surface_height = lax.fori_loop(0, BT_SUB, barotropic, surface_height)
        column_state = baroclinic_column(
            column_state,
            ocean_mask,
            ocn_operator,
            weight_total,
            marine_diffusivity_profile,
            forcing,
        )
    surface = jnp.stack(
        [column_state[0, 0], column_state[1, 0], column_state[2, 0], ocean_mask]
    ).reshape(NBACK, ocn_blocks, BLOCK)
    pieces = jnp.einsum(
        "brao,fbo->fbra", interpolation_factor_array, surface, precision=highest
    ).reshape(NBACK, ocn_blocks * REFS, BLOCK)
    target = jnp.where(
        offset == devices - 1,
        local_block,
        jnp.where(offset == 0, atm_blocks + local_block, 2 * atm_blocks + local_block),
    )
    place_table = (target[:, None] == jnp.arange(3 * atm_blocks, dtype=jnp.int32)[None, :]).astype(
        jnp.float32
    )
    collected = jnp.einsum("mt,fmc->ftc", place_table, pieces, precision=highest)
    outgoing = jnp.concatenate([collected[:, :atm_blocks], collected[:, 2 * atm_blocks :]], axis=1)
    returned = with_halo(outgoing, (("col", 1),), atm_blocks)
    totals = (
        collected[:, atm_blocks : 2 * atm_blocks]
        + returned[:, :atm_blocks]
        + returned[:, 3 * atm_blocks :]
    )
    reply_skin_values = totals.reshape(NBACK, atm_cells)
    marine_share = 1.0 + reply_skin_values[3]
    skin_upon_air_grid = jnp.stack(
        [
            (air_observed_warmth + reply_skin_values[0]) / marine_share,
            reply_skin_values[1] / marine_share,
            reply_skin_values[2] / marine_share,
        ]
    )
    return (atm_now, column_state, surface_height, skin_upon_air_grid)


def solution(mesh):
    in_specs = (
        P(None, None, ("member", "col")),
        P(("member", "col")),
        P(None, "col"),
        P(),
        P(None, None, ("member", "col")),
        P(("member", "col")),
        P(None, "col"),
        P(None, "col"),
        P("col"),
        P(),
        P(),
        P("col", None, None, None),
    )
    out_specs = (
        P(None, None, ("member", "col")),
        P(None, None, ("member", "col")),
        P(("member", "col")),
        P(None, ("member", "col")),
    )
    return jax.shard_map(body, mesh=mesh, in_specs=in_specs, out_specs=out_specs, check_vma=False)
```

profile of v0, /device:TPU:0, one launch (start us, length us, event | category | flops | bytes accessed | tf_op | source)
XLA Modules:
  0.0 372.1 jit_solution(4953704685873262440)
XLA Ops:
  3.1 5.4 %collective-permute-start.15 = (f32[4,2048]{1,0:T(4,128)}, f32[4,2048]{1,0:T(4,128)S(1)}, u32[]{:S(2)}, u32[]{:S(2)}) collective-permute-start(f32[4,2048]{1,0:T(4,128)} %pad_maximum_fusion.6), channel_id=1, source_target_pairs={{1,0},{2,1},{3,2},{4,3},{5,4},{6,5},{7,6},{8,7},{9,8},{10,9},{11,1... | collective-permute-start | bytes 98312 | tf_op jit(solution)/shard_map/ppermute | solution.py:28
  10.2 4.4 %collective-permute-start.5 = (f32[3,72,128]{2,1,0:T(8,128)}, f32[3,72,128]{2,1,0:T(8,128)}, u32[]{:S(2)}, u32[]{:S(2)}) collective-permute-start(f32[3,72,128]{2,1,0:T(8,128)} %get-tuple-element.302), channel_id=1, source_target_pairs={{1,0},{2,1},{3,2},{4,3},{5,4},{6,5},{7,6},{8,7},{9,8},{10,9},{11,1... | collective-permute-start | bytes 331784 | tf_op jit(solution)/shard_map/ppermute | solution.py:28
  21.0 4.5 %collective-permute-start.13 = (f32[3,80,128]{2,1,0:T(8,128)}, f32[3,80,128]{2,1,0:T(8,128)S(1)}, u32[]{:S(2)}, u32[]{:S(2)}) collective-permute-start(f32[3,80,128]{2,1,0:T(8,128)} %get-tuple-element.306), channel_id=1, source_target_pairs={{1,0},{2,1},{3,2},{4,3},{5,4},{6,5},{7,6},{8,7},{9,8},{10,9},{11,1... | collective-permute-start | bytes 368648 | tf_op jit(solution)/shard_map/ppermute | solution.py:28
  39.8 7.5 %fusion.147 = f32[216,16,128]{2,0,1:T(8,128)S(1)} fusion(f32[216,16,128]{2,0,1:T(8,128)S(1)} %copy.76, f32[216,16,128]{2,0,1:T(8,128)S(1)} %copy.75, f32[216,16,128]{2,0,1:T(8,128)S(1)} %copy.74, s32[16,128]{1,0:T(8,128)S(1)} %copy-done.19, s32[16,128]{1,0:T(8,128)S(1)} %copy-done.22, s32[16,128]{1,0:T(8,128)S(1)} %copy-done.25, ...), kind=kOutput, calls=%fused_computation.177 | convolution fusion | flops 2049736704 | bytes 7110656 | tf_op jit(solution)/shard_map/rbw,bwo->rbo/dot_general | solution.py:67
  51.7 5.3 %fusion.97 = f32[3,72,2048]{2,1,0:T(8,128)S(1)} fusion(f32[3,72,2048]{2,1,0:T(8,128)} %param.20, f32[3,72,2048]{2,1,0:T(8,128)} %reshape.426, f32[72,72]{1,0:T(8,128)S(1)} %copy-done.9), kind=kOutput, calls=%fused_computation.122 | convolution fusion | flops 386629632 | bytes 5329152 | tf_op jit(solution)/shard_map/lm,fmc->flc/dot_general | solution.py:74
  58.9 4.4 %collective-permute-start.7 = (f32[3,72,128]{2,1,0:T(8,128)}, f32[3,72,128]{2,1,0:T(8,128)}, u32[]{:S(2)}, u32[]{:S(2)}) collective-permute-start(f32[3,72,128]{2,1,0:T(8,128)} %get-tuple-element.300), channel_id=1, source_target_pairs={{1,0},{2,1},{3,2},{4,3},{5,4},{6,5},{7,6},{8,7},{9,8},{10,9},{11,1... | collective-permute-start | bytes 331784 | tf_op jit(solution)/shard_map/ppermute | solution.py:28
  80.7 4.4 %collective-permute-start.17 = (f32[3,80,128]{2,1,0:T(8,128)}, f32[3,80,128]{2,1,0:T(8,128)S(1)}, u32[]{:S(2)}, u32[]{:S(2)}) collective-permute-start(f32[3,80,128]{2,1,0:T(8,128)} %get-tuple-element.304), channel_id=1, source_target_pairs={{1,0},{2,1},{3,2},{4,3},{5,4},{6,5},{7,6},{8,7},{9,8},{10,9},{11,1... | collective-permute-start | bytes 368648 | tf_op jit(solution)/shard_map/ppermute | solution.py:28
  96.9 7.5 %fusion.144 = f32[216,16,128]{2,0,1:T(8,128)S(1)} fusion(f32[216,16,128]{2,0,1:T(8,128)S(1)} %copy.79, f32[216,16,128]{2,0,1:T(8,128)S(1)} %copy.78, f32[216,16,128]{2,0,1:T(8,128)S(1)} %copy.77, s32[16,128]{1,0:T(8,128)S(1)} %copy-done.20, s32[16,128]{1,0:T(8,128)S(1)} %copy-done.23, s32[16,128]{1,0:T(8,128)S(1)} %copy-done.26, s32[16,128]{1,0:T(8,128)S(1)} %copy-done.17), kind=kOutput, calls=%fused_computation.176 | convolution fusion | flops 2049736704 | bytes 7110656 | tf_op jit(solution)/shard_map/rbw,bwo->rbo/dot_general | solution.py:67
  109.0 6.6 %fusion.96 = f32[3,72,2048]{2,1,0:T(8,128)} fusion(f32[3,72,2048]{2,1,0:T(8,128)} %copy-done.3, f32[3,72,2048]{2,1,0:T(8,128)} %reshape.428, f32[72,72]{1,0:T(8,128)S(1)} %copy-done.9), kind=kOutput, calls=%fused_computation.120 | convolution fusion | flops 386629632 | bytes 5329152 | tf_op jit(solution)/shard_map/lm,fmc->flc/dot_general | solution.py:74
  136.6 4.5 %collective-permute-start.19 = (f32[4,16,128]{2,1,0:T(8,128)S(1)}, f32[4,16,128]{2,1,0:T(8,128)S(1)}, u32[]{:S(2)}, u32[]{:S(2)}) collective-permute-start(f32[4,16,128]{2,1,0:T(8,128)S(1)} %get-tuple-element.308), channel_id=1, source_target_pairs={{1,0},{2,1},{3,2},{4,3},{5,4},{6,5},{7,6},{8,7},{9,8},{10,9},{11,1... | collective-permute-start | bytes 98312 | tf_op jit(solution)/shard_map/ppermute | solution.py:28
  142.1 4.5 %collective-permute-start.9 = (f32[3,72,128]{2,1,0:T(8,128)S(1)}, f32[3,72,128]{2,1,0:T(8,128)S(1)}, u32[]{:S(2)}, u32[]{:S(2)}) collective-permute-start(f32[3,72,128]{2,1,0:T(8,128)S(1)} %get-tuple-element.298), channel_id=1, source_target_pairs={{1,0},{2,1},{3,2},{4,3},{5,4},{6,5},{7,6},{8,7},{9,8},{10,9},{11,1... | collective-permute-start | bytes 331784 | tf_op jit(solution)/shard_map/ppermute | solution.py:28
  148.9 4.7 %collective-permute-done.8 = f32[3,72,128]{2,1,0:T(8,128)S(1)} collective-permute-done((f32[3,72,128]{2,1,0:T(8,128)S(1)}, f32[3,72,128]{2,1,0:T(8,128)S(1)}, u32[]{:S(2)}, u32[]{:S(2)}) %collective-permute-start.8) | collective-permute-done | bytes 110624 | tf_op jit(solution)/shard_map/ppermute | solution.py:27
  162.5 7.4 %fusion.141 = f32[216,16,128]{2,0,1:T(8,128)S(1)} fusion(f32[216,16,128]{2,0,1:T(8,128)S(1)} %copy.82, f32[216,16,128]{2,0,1:T(8,128)S(1)} %copy.81, f32[216,16,128]{2,0,1:T(8,128)S(1)} %copy.80, s32[16,128]{1,0:T(8,128)S(1)} %copy-done.21, s32[16,128]{1,0:T(8,128)S(1)} %copy-done.24, s32[16,128]{1,0:T(8,128)S(1)} %copy-done.27, s32[16,128]{1,0:T(8,128)S(1)} %copy-done.18), kind=kOutput, calls=%fused_computation.175 | convolution fusion | flops 2049736704 | bytes 7110656 | tf_op jit(solution)/shard_map/rbw,bwo->rbo/dot_general | solution.py:67
  181.1 4.6 %collective-permute-done.10 = f32[3,72,128]{2,1,0:T(8,128)S(1)} collective-permute-done((f32[3,72,128]{2,1,0:T(8,128)S(1)}, f32[3,72,128]{2,1,0:T(8,128)S(1)}, u32[]{:S(2)}, u32[]{:S(2)}) %collective-permute-start.10) | collective-permute-done | bytes 110624 | tf_op jit(solution)/shard_map/ppermute | solution.py:27
  192.9 7.4 %fusion.138 = f32[216,16,128]{2,0,1:T(8,128)S(1)} fusion(f32[216,16,128]{2,0,1:T(8,128)S(1)} %copy.85, f32[216,16,128]{2,0,1:T(8,128)S(1)} %copy.84, f32[216,16,128]{2,0,1:T(8,128)S(1)} %copy.83, s32[16,128]{1,0:T(8,128)S(1)} %copy-done.21, s32[16,128]{1,0:T(8,128)S(1)} %copy-done.24, s32[16,128]{1,0:T(8,128)S(1)} %copy-done.27, s32[16,128]{1,0:T(8,128)S(1)} %copy-done.18), kind=kOutput, calls=%fused_computation.174 | convolution fusion | flops 2049736704 | bytes 7110656 | tf_op jit(solution)/shard_map/rbw,bwo->rbo/dot_general | solution.py:67
  204.9 5.5 %fusion.94 = f32[3,72,2048]{2,1,0:T(8,128)} fusion(f32[3,72,2048]{2,1,0:T(8,128)S(1)} %copy-done.5, f32[3,72,2048]{2,1,0:T(8,128)} %reshape.432, f32[72,72]{1,0:T(8,128)S(1)} %copy-done.9), kind=kOutput, calls=%fused_computation.116 | convolution fusion | flops 386629632 | bytes 5329152 | tf_op jit(solution)/shard_map/lm,fmc->flc/dot_general | solution.py:74
  210.4 79.8 %while.24 = (s32[]{:T(128)}, f32[1024]{0:T(1024)S(1)}, f32[1024]{0:T(1024)S(1)}, f32[1024]{0:T(1024)S(1)}, f32[1024]{0:T(1024)S(1)}, /*index=5*/s32[8,128]{1,0:T...) while((s32[]{:T(128)}, f32[1024]{0:T(1024)S(1)}, ...), condition=%wide.region_2.3_spmd.clone, body=%wide.region_1.2_spmd.clone.sunk | while | flops 11417090 | bytes 155893 | solution.py:159
  219.7 4.4 %collective-permute-done.1 = f32[128]{0:T(128)S(1)} collective-permute-done((f32[128]{0:T(128)S(1)}, f32[128]{0:T(128)S(1)}, u32[]{:S(2)}, u32[]{:S(2)}) %collective-permute-start.1) | collective-permute-done | bytes 544 | tf_op jit(solution)/shard_map/while/body/eval_jaxpr/ppermute | solution.py:27
  227.7 4.4 %collective-permute-done.1 = f32[128]{0:T(128)S(1)} collective-permute-done((f32[128]{0:T(128)S(1)}, f32[128]{0:T(128)S(1)}, u32[]{:S(2)}, u32[]{:S(2)}) %collective-permute-start.1) | collective-permute-done | bytes 544 | tf_op jit(solution)/shard_map/while/body/eval_jaxpr/ppermute | solution.py:27
  235.7 4.4 %collective-permute-done.1 = f32[128]{0:T(128)S(1)} collective-permute-done((f32[128]{0:T(128)S(1)}, f32[128]{0:T(128)S(1)}, u32[]{:S(2)}, u32[]{:S(2)}) %collective-permute-start.1) | collective-permute-done | bytes 544 | tf_op jit(solution)/shard_map/while/body/eval_jaxpr/ppermute | solution.py:27
  243.7 4.4 %collective-permute-done.1 = f32[128]{0:T(128)S(1)} collective-permute-done((f32[128]{0:T(128)S(1)}, f32[128]{0:T(128)S(1)}, u32[]{:S(2)}, u32[]{:S(2)}) %collective-permute-start.1) | collective-permute-done | bytes 544 | tf_op jit(solution)/shard_map/while/body/eval_jaxpr/ppermute | solution.py:27
  251.7 4.4 %collective-permute-done.1 = f32[128]{0:T(128)S(1)} collective-permute-done((f32[128]{0:T(128)S(1)}, f32[128]{0:T(128)S(1)}, u32[]{:S(2)}, u32[]{:S(2)}) %collective-permute-start.1) | collective-permute-done | bytes 544 | tf_op jit(solution)/shard_map/while/body/eval_jaxpr/ppermute | solution.py:27
  267.6 4.4 %collective-permute-done.1 = f32[128]{0:T(128)S(1)} collective-permute-done((f32[128]{0:T(128)S(1)}, f32[128]{0:T(128)S(1)}, u32[]{:S(2)}, u32[]{:S(2)}) %collective-permute-start.1) | collective-permute-done | bytes 544 | tf_op jit(solution)/shard_map/while/body/eval_jaxpr/ppermute | solution.py:27
  275.6 4.4 %collective-permute-done.1 = f32[128]{0:T(128)S(1)} collective-permute-done((f32[128]{0:T(128)S(1)}, f32[128]{0:T(128)S(1)}, u32[]{:S(2)}, u32[]{:S(2)}) %collective-permute-start.1) | collective-permute-done | bytes 544 | tf_op jit(solution)/shard_map/while/body/eval_jaxpr/ppermute | solution.py:27
  283.6 4.4 %collective-permute-done.1 = f32[128]{0:T(128)S(1)} collective-permute-done((f32[128]{0:T(128)S(1)}, f32[128]{0:T(128)S(1)}, u32[]{:S(2)}, u32[]{:S(2)}) %collective-permute-start.1) | collective-permute-done | bytes 544 | tf_op jit(solution)/shard_map/while/body/eval_jaxpr/ppermute | solution.py:27
  290.2 79.9 %while.25 = (s32[]{:T(128)}, f32[1024]{0:T(1024)S(1)}, f32[1024]{0:T(1024)S(1)}, f32[1024]{0:T(1024)S(1)}, f32[1024]{0:T(1024)S(1)}, /*index=5*/s32[8,128]{1,0:T...) while((s32[]{:T(128)}, f32[1024]{0:T(1024)S(1)}, ...), condition=%wide.region_4.5_spmd.clone, body=%wide.region_3.4_spmd.clone.sunk | while | flops 11417090 | bytes 155893 | solution.py:159
  291.6 4.4 %collective-permute-done.3 = f32[128]{0:T(128)S(1)} collective-permute-done((f32[128]{0:T(128)S(1)}, f32[128]{0:T(128)S(1)}, u32[]{:S(2)}, u32[]{:S(2)}) %collective-permute-start.3) | collective-permute-done | bytes 544 | tf_op jit(solution)/shard_map/while/body/eval_jaxpr/ppermute | solution.py:27
  307.6 4.4 %collective-permute-done.3 = f32[128]{0:T(128)S(1)} collective-permute-done((f32[128]{0:T(128)S(1)}, f32[128]{0:T(128)S(1)}, u32[]{:S(2)}, u32[]{:S(2)}) %collective-permute-start.3) | collective-permute-done | bytes 544 | tf_op jit(solution)/shard_map/while/body/eval_jaxpr/ppermute | solution.py:27
  315.6 4.4 %collective-permute-done.3 = f32[128]{0:T(128)S(1)} collective-permute-done((f32[128]{0:T(128)S(1)}, f32[128]{0:T(128)S(1)}, u32[]{:S(2)}, u32[]{:S(2)}) %collective-permute-start.3) | collective-permute-done | bytes 544 | tf_op jit(solution)/shard_map/while/body/eval_jaxpr/ppermute | solution.py:27
  323.6 4.4 %collective-permute-done.3 = f32[128]{0:T(128)S(1)} collective-permute-done((f32[128]{0:T(128)S(1)}, f32[128]{0:T(128)S(1)}, u32[]{:S(2)}, u32[]{:S(2)}) %collective-permute-start.3) | collective-permute-done | bytes 544 | tf_op jit(solution)/shard_map/while/body/eval_jaxpr/ppermute | solution.py:27
  331.6 4.4 %collective-permute-done.3 = f32[128]{0:T(128)S(1)} collective-permute-done((f32[128]{0:T(128)S(1)}, f32[128]{0:T(128)S(1)}, u32[]{:S(2)}, u32[]{:S(2)}) %collective-permute-start.3) | collective-permute-done | bytes 544 | tf_op jit(solution)/shard_map/while/body/eval_jaxpr/ppermute | solution.py:27
  347.6 4.4 %collective-permute-done.3 = f32[128]{0:T(128)S(1)} collective-permute-done((f32[128]{0:T(128)S(1)}, f32[128]{0:T(128)S(1)}, u32[]{:S(2)}, u32[]{:S(2)}) %collective-permute-start.3) | collective-permute-done | bytes 544 | tf_op jit(solution)/shard_map/while/body/eval_jaxpr/ppermute | solution.py:27
  (413 shorter events, 218.4 us)
Async XLA Ops:
  3.1 22.3 %collective-permute-start.15 = (f32[4,2048]{1,0:T(4,128)}, f32[4,2048]{1,0:T(4,128)S(1)}, u32[]{:S(2)}, u32[]{:S(2)}) collective-permute-start(f32[4,2048]{1,0:T(4,128)} %pad_maximum_fusion.6), channel_id=1, source_target_pairs={{1,0},{2,1},{3,2},{4,3},{5,4},{6,5},{7,6},{8,7},{9,8},{10,9},{11,1... | collective-permute-start | bytes 98312 | tf_op jit(solution)/shard_map/ppermute | solution.py:28
  8.6 17.5 %collective-permute-start.14 = (f32[4,2048]{1,0:T(4,128)}, f32[4,2048]{1,0:T(4,128)}, u32[]{:S(2)}, u32[]{:S(2)}) collective-permute-start(f32[4,2048]{1,0:T(4,128)} %pad_maximum_fusion.6), channel_id=1, source_target_pairs={{0,1},{1,2},{2,3},{3,4},{4,5},{5,6},{6,7},{7,8},{8,9},{9,10},{10,1... | collective-permute-start | bytes 98312 | tf_op jit(solution)/shard_map/ppermute | solution.py:27
  10.2 18.1 %collective-permute-start.5 = (f32[3,72,128]{2,1,0:T(8,128)}, f32[3,72,128]{2,1,0:T(8,128)}, u32[]{:S(2)}, u32[]{:S(2)}) collective-permute-start(f32[3,72,128]{2,1,0:T(8,128)} %get-tuple-element.302), channel_id=1, source_target_pairs={{1,0},{2,1},{3,2},{4,3},{5,4},{6,5},{7,6},{8,7},{9,8},{10,9},{11,1... | collective-permute-start | bytes 331784 | tf_op jit(solution)/shard_map/ppermute | solution.py:28
  14.7 13.7 %collective-permute-start.4 = (f32[3,72,128]{2,1,0:T(8,128)}, f32[3,72,128]{2,1,0:T(8,128)}, u32[]{:S(2)}, u32[]{:S(2)}) collective-permute-start(f32[3,72,128]{2,1,0:T(8,128)} %get-tuple-element.301), channel_id=1, source_target_pairs={{0,1},{1,2},{2,3},{3,4},{4,5},{5,6},{6,7},{7,8},{8,9},{9,10},{10,1... | collective-permute-start | bytes 331784 | tf_op jit(solution)/shard_map/ppermute | solution.py:27
  21.0 42.4 %collective-permute-start.13 = (f32[3,80,128]{2,1,0:T(8,128)}, f32[3,80,128]{2,1,0:T(8,128)S(1)}, u32[]{:S(2)}, u32[]{:S(2)}) collective-permute-start(f32[3,80,128]{2,1,0:T(8,128)} %get-tuple-element.306), channel_id=1, source_target_pairs={{1,0},{2,1},{3,2},{4,3},{5,4},{6,5},{7,6},{8,7},{9,8},{10,9},{11,1... | collective-permute-start | bytes 368648 | tf_op jit(solution)/shard_map/ppermute | solution.py:28
  26.1 37.3 %collective-permute-start.12 = (f32[3,80,128]{2,1,0:T(8,128)S(1)}, f32[3,80,128]{2,1,0:T(8,128)S(1)}, u32[]{:S(2)}, u32[]{:S(2)}) collective-permute-start(f32[3,80,128]{2,1,0:T(8,128)S(1)} %get-tuple-element.305), channel_id=1, source_target_pairs={{0,1},{1,2},{2,3},{3,4},{4,5},{5,6},{6,7},{7,8},{8,9},{9,10},{10,1... | collective-permute-start | bytes 368648 | tf_op jit(solution)/shard_map/ppermute | solution.py:27
  58.9 26.3 %collective-permute-start.7 = (f32[3,72,128]{2,1,0:T(8,128)}, f32[3,72,128]{2,1,0:T(8,128)}, u32[]{:S(2)}, u32[]{:S(2)}) collective-permute-start(f32[3,72,128]{2,1,0:T(8,128)} %get-tuple-element.300), channel_id=1, source_target_pairs={{1,0},{2,1},{3,2},{4,3},{5,4},{6,5},{7,6},{8,7},{9,8},{10,9},{11,1... | collective-permute-start | bytes 331784 | tf_op jit(solution)/shard_map/ppermute | solution.py:28
  63.4 21.8 %collective-permute-start.6 = (f32[3,72,128]{2,1,0:T(8,128)}, f32[3,72,128]{2,1,0:T(8,128)}, u32[]{:S(2)}, u32[]{:S(2)}) collective-permute-start(f32[3,72,128]{2,1,0:T(8,128)} %get-tuple-element.299), channel_id=1, source_target_pairs={{0,1},{1,2},{2,3},{3,4},{4,5},{5,6},{6,7},{7,8},{8,9},{9,10},{10,1... | collective-permute-start | bytes 331784 | tf_op jit(solution)/shard_map/ppermute | solution.py:27
  80.7 34.9 %collective-permute-start.17 = (f32[3,80,128]{2,1,0:T(8,128)}, f32[3,80,128]{2,1,0:T(8,128)S(1)}, u32[]{:S(2)}, u32[]{:S(2)}) collective-permute-start(f32[3,80,128]{2,1,0:T(8,128)} %get-tuple-element.304), channel_id=1, source_target_pairs={{1,0},{2,1},{3,2},{4,3},{5,4},{6,5},{7,6},{8,7},{9,8},{10,9},{11,1... | collective-permute-start | bytes 368648 | tf_op jit(solution)/shard_map/ppermute | solution.py:28
  85.2 30.5 %collective-permute-start.16 = (f32[3,80,128]{2,1,0:T(8,128)S(1)}, f32[3,80,128]{2,1,0:T(8,128)S(1)}, u32[]{:S(2)}, u32[]{:S(2)}) collective-permute-start(f32[3,80,128]{2,1,0:T(8,128)S(1)} %get-tuple-element.303), channel_id=1, source_target_pairs={{0,1},{1,2},{2,3},{3,4},{4,5},{5,6},{6,7},{7,8},{8,9},{9,10},{10,1... | collective-permute-start | bytes 368648 | tf_op jit(solution)/shard_map/ppermute | solution.py:27
  136.6 11.7 %collective-permute-start.19 = (f32[4,16,128]{2,1,0:T(8,128)S(1)}, f32[4,16,128]{2,1,0:T(8,128)S(1)}, u32[]{:S(2)}, u32[]{:S(2)}) collective-permute-start(f32[4,16,128]{2,1,0:T(8,128)S(1)} %get-tuple-element.308), channel_id=1, source_target_pairs={{1,0},{2,1},{3,2},{4,3},{5,4},{6,5},{7,6},{8,7},{9,8},{10,9},{11,1... | collective-permute-start | bytes 98312 | tf_op jit(solution)/shard_map/ppermute | solution.py:28
  141.1 7.2 %collective-permute-start.18 = (f32[4,16,128]{2,1,0:T(8,128)S(1)}, f32[4,16,128]{2,1,0:T(8,128)S(1)}, u32[]{:S(2)}, u32[]{:S(2)}) collective-permute-start(f32[4,16,128]{2,1,0:T(8,128)S(1)} %get-tuple-element.307), channel_id=1, source_target_pairs={{0,1},{1,2},{2,3},{3,4},{4,5},{5,6},{6,7},{7,8},{8,9},{9,10},{10,1... | collective-permute-start | bytes 98312 | tf_op jit(solution)/shard_map/ppermute | solution.py:27
  142.1 6.8 %collective-permute-start.9 = (f32[3,72,128]{2,1,0:T(8,128)S(1)}, f32[3,72,128]{2,1,0:T(8,128)S(1)}, u32[]{:S(2)}, u32[]{:S(2)}) collective-permute-start(f32[3,72,128]{2,1,0:T(8,128)S(1)} %get-tuple-element.298), channel_id=1, source_target_pairs={{1,0},{2,1},{3,2},{4,3},{5,4},{6,5},{7,6},{8,7},{9,8},{10,9},{11,1... | collective-permute-start | bytes 331784 | tf_op jit(solution)/shard_map/ppermute | solution.py:28
  146.6 7.0 %collective-permute-start.8 = (f32[3,72,128]{2,1,0:T(8,128)S(1)}, f32[3,72,128]{2,1,0:T(8,128)S(1)}, u32[]{:S(2)}, u32[]{:S(2)}) collective-permute-start(f32[3,72,128]{2,1,0:T(8,128)S(1)} %get-tuple-element.297), channel_id=1, source_target_pairs={{0,1},{1,2},{2,3},{3,4},{4,5},{5,6},{6,7},{7,8},{8,9},{9,10},{10,1... | collective-permute-start | bytes 331784 | tf_op jit(solution)/shard_map/ppermute | solution.py:27
  178.7 6.9 %collective-permute-start.10 = (f32[3,72,128]{2,1,0:T(8,128)S(1)}, f32[3,72,128]{2,1,0:T(8,128)S(1)}, u32[]{:S(2)}, u32[]{:S(2)}) collective-permute-start(f32[3,72,128]{2,1,0:T(8,128)S(1)} %get-tuple-element.295), channel_id=1, source_target_pairs={{0,1},{1,2},{2,3},{3,4},{4,5},{5,6},{6,7},{7,8},{8,9},{9,10},{10,1... | collective-permute-start | bytes 331784 | tf_op jit(solution)/shard_map/ppermute | solution.py:27
  210.4 5.7 %collective-permute-start.1 = (f32[128]{0:T(128)S(1)}, f32[128]{0:T(128)S(1)}, u32[]{:S(2)}, u32[]{:S(2)}) collective-permute-start(f32[128]{0:T(128)S(1)} %get-tuple-element.536), channel_id=1, source_target_pairs={{0,1},{1,2},{2,3},{3,4},{4,5},{5,6},{6,7},{7,8},{8,9},{9,10},{10,1... | collective-permute-start | bytes 1544 | tf_op jit(solution)/shard_map/while/body/eval_jaxpr/ppermute | solution.py:27
  218.4 5.7 %collective-permute-start.1 = (f32[128]{0:T(128)S(1)}, f32[128]{0:T(128)S(1)}, u32[]{:S(2)}, u32[]{:S(2)}) collective-permute-start(f32[128]{0:T(128)S(1)} %get-tuple-element.536), channel_id=1, source_target_pairs={{0,1},{1,2},{2,3},{3,4},{4,5},{5,6},{6,7},{7,8},{8,9},{9,10},{10,1... | collective-permute-start | bytes 1544 | tf_op jit(solution)/shard_map/while/body/eval_jaxpr/ppermute | solution.py:27
  226.4 5.7 %collective-permute-start.1 = (f32[128]{0:T(128)S(1)}, f32[128]{0:T(128)S(1)}, u32[]{:S(2)}, u32[]{:S(2)}) collective-permute-start(f32[128]{0:T(128)S(1)} %get-tuple-element.536), channel_id=1, source_target_pairs={{0,1},{1,2},{2,3},{3,4},{4,5},{5,6},{6,7},{7,8},{8,9},{9,10},{10,1... | collective-permute-start | bytes 1544 | tf_op jit(solution)/shard_map/while/body/eval_jaxpr/ppermute | solution.py:27
  234.4 5.7 %collective-permute-start.1 = (f32[128]{0:T(128)S(1)}, f32[128]{0:T(128)S(1)}, u32[]{:S(2)}, u32[]{:S(2)}) collective-permute-start(f32[128]{0:T(128)S(1)} %get-tuple-element.536), channel_id=1, source_target_pairs={{0,1},{1,2},{2,3},{3,4},{4,5},{5,6},{6,7},{7,8},{8,9},{9,10},{10,1... | collective-permute-start | bytes 1544 | tf_op jit(solution)/shard_map/while/body/eval_jaxpr/ppermute | solution.py:27
  242.4 5.7 %collective-permute-start.1 = (f32[128]{0:T(128)S(1)}, f32[128]{0:T(128)S(1)}, u32[]{:S(2)}, u32[]{:S(2)}) collective-permute-start(f32[128]{0:T(128)S(1)} %get-tuple-element.536), channel_id=1, source_target_pairs={{0,1},{1,2},{2,3},{3,4},{4,5},{5,6},{6,7},{7,8},{8,9},{9,10},{10,1... | collective-permute-start | bytes 1544 | tf_op jit(solution)/shard_map/while/body/eval_jaxpr/ppermute | solution.py:27
  250.4 5.7 %collective-permute-start.1 = (f32[128]{0:T(128)S(1)}, f32[128]{0:T(128)S(1)}, u32[]{:S(2)}, u32[]{:S(2)}) collective-permute-start(f32[128]{0:T(128)S(1)} %get-tuple-element.536), channel_id=1, source_target_pairs={{0,1},{1,2},{2,3},{3,4},{4,5},{5,6},{6,7},{7,8},{8,9},{9,10},{10,1... | collective-permute-start | bytes 1544 | tf_op jit(solution)/shard_map/while/body/eval_jaxpr/ppermute | solution.py:27
  266.4 5.7 %collective-permute-start.1 = (f32[128]{0:T(128)S(1)}, f32[128]{0:T(128)S(1)}, u32[]{:S(2)}, u32[]{:S(2)}) collective-permute-start(f32[128]{0:T(128)S(1)} %get-tuple-element.536), channel_id=1, source_target_pairs={{0,1},{1,2},{2,3},{3,4},{4,5},{5,6},{6,7},{7,8},{8,9},{9,10},{10,1... | collective-permute-start | bytes 1544 | tf_op jit(solution)/shard_map/while/body/eval_jaxpr/ppermute | solution.py:27
  274.3 5.7 %collective-permute-start.1 = (f32[128]{0:T(128)S(1)}, f32[128]{0:T(128)S(1)}, u32[]{:S(2)}, u32[]{:S(2)}) collective-permute-start(f32[128]{0:T(128)S(1)} %get-tuple-element.536), channel_id=1, source_target_pairs={{0,1},{1,2},{2,3},{3,4},{4,5},{5,6},{6,7},{7,8},{8,9},{9,10},{10,1... | collective-permute-start | bytes 1544 | tf_op jit(solution)/shard_map/while/body/eval_jaxpr/ppermute | solution.py:27
  282.3 5.7 %collective-permute-start.1 = (f32[128]{0:T(128)S(1)}, f32[128]{0:T(128)S(1)}, u32[]{:S(2)}, u32[]{:S(2)}) collective-permute-start(f32[128]{0:T(128)S(1)} %get-tuple-element.536), channel_id=1, source_target_pairs={{0,1},{1,2},{2,3},{3,4},{4,5},{5,6},{6,7},{7,8},{8,9},{9,10},{10,1... | collective-permute-start | bytes 1544 | tf_op jit(solution)/shard_map/while/body/eval_jaxpr/ppermute | solution.py:27
  290.3 5.7 %collective-permute-start.3 = (f32[128]{0:T(128)S(1)}, f32[128]{0:T(128)S(1)}, u32[]{:S(2)}, u32[]{:S(2)}) collective-permute-start(f32[128]{0:T(128)S(1)} %get-tuple-element.558), channel_id=1, source_target_pairs={{0,1},{1,2},{2,3},{3,4},{4,5},{5,6},{6,7},{7,8},{8,9},{9,10},{10,1... | collective-permute-start | bytes 1544 | tf_op jit(solution)/shard_map/while/body/eval_jaxpr/ppermute | solution.py:27
  306.3 5.7 %collective-permute-start.3 = (f32[128]{0:T(128)S(1)}, f32[128]{0:T(128)S(1)}, u32[]{:S(2)}, u32[]{:S(2)}) collective-permute-start(f32[128]{0:T(128)S(1)} %get-tuple-element.558), channel_id=1, source_target_pairs={{0,1},{1,2},{2,3},{3,4},{4,5},{5,6},{6,7},{7,8},{8,9},{9,10},{10,1... | collective-permute-start | bytes 1544 | tf_op jit(solution)/shard_map/while/body/eval_jaxpr/ppermute | solution.py:27
  314.3 5.7 %collective-permute-start.3 = (f32[128]{0:T(128)S(1)}, f32[128]{0:T(128)S(1)}, u32[]{:S(2)}, u32[]{:S(2)}) collective-permute-start(f32[128]{0:T(128)S(1)} %get-tuple-element.558), channel_id=1, source_target_pairs={{0,1},{1,2},{2,3},{3,4},{4,5},{5,6},{6,7},{7,8},{8,9},{9,10},{10,1... | collective-permute-start | bytes 1544 | tf_op jit(solution)/shard_map/while/body/eval_jaxpr/ppermute | solution.py:27
  322.3 5.7 %collective-permute-start.3 = (f32[128]{0:T(128)S(1)}, f32[128]{0:T(128)S(1)}, u32[]{:S(2)}, u32[]{:S(2)}) collective-permute-start(f32[128]{0:T(128)S(1)} %get-tuple-element.558), channel_id=1, source_target_pairs={{0,1},{1,2},{2,3},{3,4},{4,5},{5,6},{6,7},{7,8},{8,9},{9,10},{10,1... | collective-permute-start | bytes 1544 | tf_op jit(solution)/shard_map/while/body/eval_jaxpr/ppermute | solution.py:27
  330.3 5.7 %collective-permute-start.3 = (f32[128]{0:T(128)S(1)}, f32[128]{0:T(128)S(1)}, u32[]{:S(2)}, u32[]{:S(2)}) collective-permute-start(f32[128]{0:T(128)S(1)} %get-tuple-element.558), channel_id=1, source_target_pairs={{0,1},{1,2},{2,3},{3,4},{4,5},{5,6},{6,7},{7,8},{8,9},{9,10},{10,1... | collective-permute-start | bytes 1544 | tf_op jit(solution)/shard_map/while/body/eval_jaxpr/ppermute | solution.py:27
  338.3 5.7 %collective-permute-start.3 = (f32[128]{0:T(128)S(1)}, f32[128]{0:T(128)S(1)}, u32[]{:S(2)}, u32[]{:S(2)}) collective-permute-start(f32[128]{0:T(128)S(1)} %get-tuple-element.558), channel_id=1, source_target_pairs={{0,1},{1,2},{2,3},{3,4},{4,5},{5,6},{6,7},{7,8},{8,9},{9,10},{10,1... | collective-permute-start | bytes 1544 | tf_op jit(solution)/shard_map/while/body/eval_jaxpr/ppermute | solution.py:27
  346.3 5.7 %collective-permute-start.3 = (f32[128]{0:T(128)S(1)}, f32[128]{0:T(128)S(1)}, u32[]{:S(2)}, u32[]{:S(2)}) collective-permute-start(f32[128]{0:T(128)S(1)} %get-tuple-element.558), channel_id=1, source_target_pairs={{0,1},{1,2},{2,3},{3,4},{4,5},{5,6},{6,7},{7,8},{8,9},{9,10},{10,1... | collective-permute-start | bytes 1544 | tf_op jit(solution)/shard_map/while/body/eval_jaxpr/ppermute | solution.py:27
  362.3 5.7 %collective-permute-start.3 = (f32[128]{0:T(128)S(1)}, f32[128]{0:T(128)S(1)}, u32[]{:S(2)}, u32[]{:S(2)}) collective-permute-start(f32[128]{0:T(128)S(1)} %get-tuple-element.558), channel_id=1, source_target_pairs={{0,1},{1,2},{2,3},{3,4},{4,5},{5,6},{6,7},{7,8},{8,9},{9,10},{10,1... | collective-permute-start | bytes 1544 | tf_op jit(solution)/shard_map/while/body/eval_jaxpr/ppermute | solution.py:27
  (79 other events, 313.6 us)
where the time goes:
time: 376 us; the launch traced here: 372 us
  waiting for transfers between devices  115 us (31%)
  matrix products  112 us (30%)
  local copies, waits for them, and re-layouts  80.1 us (21%)
  starting transfers between devices  44 us (12%)
  other arithmetic  17.5 us (5%)
    ppermute x28, waiting for transfers between devices, with_halo(): before = lax.ppermute(last, axis, up)  97.8 us
    dot_general x26, matrix products, apply_operator(): result = jnp.einsum('rbw,bwo->rbo', windows, operator, precision=highest)  80.7 us
    ppermute x28, starting transfers between devices, with_halo(): after = lax.ppermute(initial, axis, down)  33.4 us
    dot_general x4, matrix products, atm_update(): jnp.einsum('lm,fmc->flc', mixing, blended, precision=highest)  21.7 us
    slice x26, local copies, waits for them, and re-layouts, apply_operator(): flat[:, part:part + blocks]  20 us
    ppermute x28, waiting for transfers between devices, with_halo(): after = lax.ppermute(initial, axis, down)  17.5 us
    reshape x6, local copies, waits for them, and re-layouts, apply_operator(): flat = extended.reshape((-1, length // BLOCK, BLOCK))  15.4 us
    reshape x6, local copies, waits for them, and re-layouts, apply_operator(): return result.reshape(lead + (blocks * BLOCK,))  15 us
  transfers between devices with their start and end apart: 56, of which 44 were waited for; matrix products, arithmetic and copies ran while one was open for 24% of the time, Pallas kernels for 0%

commit v1 on v0

v1 whole, which is shorter than its diff:
```python
import functools

import jax
import jax.numpy as jnp
from jax import lax
from jax.experimental import pallas as pl
from jax.experimental.pallas import tpu as pltpu
from jax.sharding import PartitionSpec as P

BLOCK = 128
SUB_A = 4
BT_SUB = 10
BC_SUB = 2
MESH = pl.DeviceIdType.MESH
F32 = jnp.float32
BF16 = jnp.bfloat16
HIGHEST = lax.Precision.HIGHEST
FAR = 3
HA = SUB_A * BLOCK
HO = BC_SUB * BLOCK


def iota(shape, dim):
    return lax.broadcasted_iota(jnp.int32, shape, dim)


def dot(a, b):
    return jnp.dot(a, b, preferred_element_type=F32)


def dot_exact(a, b):
    return jnp.dot(a, b, preferred_element_type=F32, precision=HIGHEST)


def pieces_of(x):
    hi = x.astype(BF16)
    return hi, (x - hi.astype(F32)).astype(BF16)


def level_operator(profile):
    n = profile.shape[0]
    return profile + jnp.where(iota((n, n), 0) == iota((n, n), 1), F32(0.6), F32(0.0))


def spread_columns(matrix, field, width):
    n = matrix.shape[0]
    place = (iota((n, width), 1) == iota((n, width), 0) + field * n).astype(F32)
    return dot_exact(matrix, place)


def gather_lanes(rows, lanes):
    return jnp.take_along_axis(rows, lanes, axis=1, mode="promise_in_bounds")


def main_kernel(
    n,
    air, warm, alist, mar, sea, mlist, mff, mind, mdiff, donor, weights,
    t_out, y_out, tot_out, ssh_out,
    low, centre, left, right, xc, xl, xr, lx, lleft, lright,
    wf, whi, wlo, cand, px, ofx, idx, coef, eta, forc, gath, op, fhi, flo,
    hla, hlb, xa, xb, pc, coll, rb,
    ss, rs, ls,
):
    levels_a = air.shape[1]
    levels_o = mar.shape[1]
    na = air.shape[2]
    no = mar.shape[2]
    ab = na // BLOCK
    ob = no // BLOCK
    rows_a = hla.shape[0] // 2
    rows_o = xa.shape[0] // 2
    refs = donor.shape[0]
    me = lax.axis_index("col")

    def peer(d):
        return {"col": lax.rem(me + d + n, n)}

    def remote(src, dst, i, d):
        return pltpu.make_async_remote_copy(
            src_ref=src, dst_ref=dst, send_sem=ss.at[i], recv_sem=rs.at[i],
            device_id=peer(d), device_id_type=MESH,
        )

    low_copy = pltpu.make_async_copy(air.at[:, levels_a - 8 :, :], low, ls.at[0])
    low_copy.start()
    w_copy = pltpu.make_async_copy(weights, wf, ls.at[1])
    air_copy = pltpu.make_async_copy(air, centre, ls.at[2])
    mar_copy = pltpu.make_async_copy(mar, xc, ls.at[3])
    w_copy.start()
    mar_copy.start()
    air_copy.start()
    far = [d for d in range(-FAR, FAR + 1) if d != 0]
    barrier = pltpu.get_barrier_semaphore()
    for d in far:
        pl.semaphore_signal(barrier, inc=1, device_id=peer(d), device_id_type=MESH)

    for b in range(ob):
        cols = slice(b * BLOCK, (b + 1) * BLOCK)
        px[FAR, 0:6, b, :] = mlist[:, cols].astype(F32)
        px[FAR, 6:12, b, :] = mff[:, cols]
    px[FAR, 12, :, :] = mind[...].astype(F32)
    px[FAR, 13, :, :] = sea[...]

    low_copy.wait()
    lowest = [low[f, 7:8, :] for f in range(3)]
    flux = jnp.concatenate(
        [
            0.5 * (lowest[0] - warm[...]),
            0.3 * lowest[1] * lowest[2],
            0.5 * lowest[1],
            0.5 * lowest[2],
        ],
        axis=0,
    )
    for b in range(ab):
        cand[ab + b] = flux[:, b * BLOCK : (b + 1) * BLOCK]

    pl.semaphore_wait(barrier, len(far))
    flux_sends = [
        remote(cand.at[ab : 2 * ab], cand.at[0:ab], 0, 1),
        remote(cand.at[ab : 2 * ab], cand.at[2 * ab : 3 * ab], 1, -1),
    ]
    table_sends = [remote(px.at[FAR], px.at[FAR - d], 2 + i, d) for i, d in enumerate(far)]
    list_sends = [
        remote(alist.at[:, na - HA : na], lleft, 8, 1),
        remote(alist.at[:, 0:HA], lright, 9, -1),
    ]
    mar_sends = [
        remote(mar.at[:, :, no - HO : no], xl, 10, 1),
        remote(mar.at[:, :, 0:HO], xr, 11, -1),
    ]
    air_sends = [
        remote(air.at[:, :, na - HA : na], left, 12, 1),
        remote(air.at[:, :, 0:HA], right, 13, -1),
    ]
    for c in flux_sends + table_sends + list_sends + mar_sends + air_sends:
        c.start()

    pairs = ab // 2 + SUB_A
    zero_block = jnp.zeros((BLOCK, BLOCK), BF16)

    def build_air(j, carry):
        op[j, 3 * BLOCK : 4 * BLOCK, 0:BLOCK] = zero_block
        op[j, 0:BLOCK, BLOCK : 2 * BLOCK] = zero_block
        for side in range(2):
            e = 2 * j + side
            b = lax.rem(e + ab - SUB_A, ab)
            links = lx[:, pl.ds(pl.multiple_of(e * BLOCK, BLOCK), BLOCK)] - b * BLOCK
            for part in range(3):
                ids = iota((BLOCK, BLOCK), 0) + part * BLOCK
                total = jnp.zeros((BLOCK, BLOCK), F32)
                for k in range(links.shape[0]):
                    total = total + jnp.where(links[k : k + 1, :] == ids, F32(1.0), F32(0.0))
                r = (part + side) * BLOCK
                op[j, r : r + BLOCK, side * BLOCK : (side + 1) * BLOCK] = total.astype(BF16)
        return carry

    lx[:, HA : HA + na] = alist[...]
    half = SUB_A // 2
    lax.fori_loop(half, pairs - half, build_air, 0)

    w_copy.wait()

    def split_weights(b, carry):
        hi, lo = pieces_of(wf[b])
        whi[b] = hi
        wlo[b] = lo
        return carry

    lax.fori_loop(0, ob, split_weights, 0)

    def place_of(b, r):
        ref = donor[r, me * ob + b]
        owner = ref // ab
        off = lax.rem(owner - me + n, n)
        base = jnp.where(off == 0, ab, jnp.where(off == 1, 2 * ab, 0))
        return base + lax.rem(ref, ab)

    for c in flux_sends:
        c.wait_recv()
    lane_ids = iota((8, BLOCK), 1)
    places = jnp.zeros((8, BLOCK), jnp.int32)
    for b in range(ob):
        picked = []
        for r in range(refs):
            where = place_of(b, r)
            places = jnp.where(lane_ids == b * refs + r, where, places)
            picked.append(cand[where])
        f = jnp.concatenate(picked, axis=1)
        hi = f.astype(BF16).astype(F32)
        stacked = jnp.concatenate([hi, f - hi], axis=0).astype(BF16)
        first = dot(stacked, whi[b])
        second = dot(stacked, wlo[b])
        ofx[FAR, :, b, :] = first[0:4] + first[4:8] + second[0:4]
    of_sends = [remote(ofx.at[FAR], ofx.at[FAR - d], 14 + i, d) for i, d in enumerate(far)]
    for c in of_sends:
        c.start()

    for c in table_sends:
        c.wait_recv()
    block_ids = iota((ob, BLOCK), 0) * BLOCK

    def prepare(s, carry):
        m = px[s, 12]
        total = jnp.zeros((ob, BLOCK), F32)
        for k in range(6):
            idx[s, k] = px[s, k].astype(jnp.int32) - block_ids
            w = px[s, 6 + k]
            total = total + w
            coef[s, k] = m * w
        coef[s, 6] = m * (1.0 - total)
        eta[pl.ds(pl.multiple_of(s * ob + 8, 8), ob), :] = m * px[s, 13]
        return carry

    slots = 2 * FAR + 1
    lax.fori_loop(0, slots, prepare, 0)
    eta[0:8, :] = jnp.zeros((8, BLOCK), F32)
    eta[8 + slots * ob : 16 + slots * ob, :] = jnp.zeros((8, BLOCK), F32)

    opairs = ob // 2 + BC_SUB

    def build_ocean(j, carry):
        for ref_ in (fhi, flo):
            ref_[j, 3 * BLOCK : 4 * BLOCK, 0:BLOCK] = zero_block
            ref_[j, 0:BLOCK, BLOCK : 2 * BLOCK] = zero_block
        for side in range(2):
            e = 2 * j + side + FAR * ob - BC_SUB
            s = e // ob
            b = lax.rem(e, ob)
            links = [idx[s, k, pl.ds(b, 1), :] for k in range(6)]
            values = [coef[s, k, pl.ds(b, 1), :] for k in range(7)]
            for part in range(3):
                ids = iota((BLOCK, BLOCK), 0) + part * BLOCK
                if part == 1:
                    own = iota((BLOCK, BLOCK), 0) == iota((BLOCK, BLOCK), 1)
                    total = jnp.where(own, values[6], F32(0.0))
                else:
                    total = jnp.zeros((BLOCK, BLOCK), F32)
                for k in range(6):
                    total = total + jnp.where(links[k] == ids, values[k], F32(0.0))
                r = (part + side) * BLOCK
                hi, lo = pieces_of(total)
                fhi[j, r : r + BLOCK, side * BLOCK : (side + 1) * BLOCK] = hi
                flo[j, r : r + BLOCK, side * BLOCK : (side + 1) * BLOCK] = lo
        return carry

    lax.fori_loop(0, opairs, build_ocean, 0)

    def put_ocean(value, at, buf):
        rows = value.reshape(rows_o, value.shape[2])
        hi, lo = pieces_of(rows)
        buf[0:rows_o, at : at + value.shape[2]] = hi
        buf[rows_o : 2 * rows_o, at : at + value.shape[2]] = lo

    edge_o = jnp.zeros((2 * rows_o, BLOCK), BF16)
    xa[:, 0:BLOCK] = edge_o
    xa[:, xa.shape[1] - BLOCK : xa.shape[1]] = edge_o
    mar_copy.wait()
    for b in range(ob):
        m = px[FAR, 12, b : b + 1, :]
        cols = slice(b * BLOCK, (b + 1) * BLOCK)
        put_ocean(xc[:, :, cols] * m, BLOCK + HO + b * BLOCK, xa)
    for c in mar_sends:
        c.wait_recv()
    for b in range(BC_SUB):
        cols = slice(b * BLOCK, (b + 1) * BLOCK)
        m = px[FAR - 1, 12, ob - BC_SUB + b : ob - BC_SUB + b + 1, :]
        put_ocean(xl[:, :, cols] * m, BLOCK + b * BLOCK, xa)
        m = px[FAR + 1, 12, b : b + 1, :]
        put_ocean(xr[:, :, cols] * m, BLOCK + HO + no + b * BLOCK, xa)

    def ocean_apply(j, src):
        window = src[:, pl.ds(pl.multiple_of(j * 2 * BLOCK, BLOCK), 4 * BLOCK)]
        a = dot(window, fhi[j])
        b = dot(window[0:rows_o], flo[j])
        return a[0:rows_o] + a[rows_o : 2 * rows_o] + b

    def ocean_first(j, carry):
        hi, lo = pieces_of(ocean_apply(j, xa))
        cols = pl.ds(pl.multiple_of(j * 2 * BLOCK + BLOCK, BLOCK), 2 * BLOCK)
        xb[0:rows_o, cols] = hi
        xb[rows_o : 2 * rows_o, cols] = lo
        return carry

    lax.fori_loop(0, opairs, ocean_first, 0)

    def ocean_second(j, carry):
        cols = pl.ds(pl.multiple_of((j - 1) * 2 * BLOCK, BLOCK), 2 * BLOCK)
        y_out[0:rows_o, cols] = ocean_apply(j, xb)
        return carry

    lax.fori_loop(1, opairs - 1, ocean_second, 0)

    for c in of_sends:
        c.wait_recv()

    def neighbours(prev, cur, after, s):
        total = coef[s, 6] * cur
        for k in range(6):
            at = idx[s, k]
            lanes = jnp.bitwise_and(at, BLOCK - 1)
            g0 = gather_lanes(prev, lanes)
            g1 = gather_lanes(cur, lanes)
            g2 = gather_lanes(after, lanes)
            g = jnp.where(at < BLOCK, g0, jnp.where(at < 2 * BLOCK, g1, g2))
            total = total + coef[s, k] * g
        return total

    gath[...] = jnp.zeros(gath.shape, F32)
    for i, field in enumerate((0, 2, 3)):
        for o in range(3):
            s = FAR - 1 + o
            forc[o * ob : (o + 1) * ob, :] = 0.2 * ofx[s, field] * px[s, 12]
        cur = forc[ob : 2 * ob, :]
        moved = neighbours(forc[ob - 1 : 2 * ob - 1, :], cur, forc[ob + 1 : 2 * ob + 1, :], FAR)
        gath[i] = moved
        gath[3 + i] = cur
    for b in range(ob):
        y_out[rows_o : rows_o + 16, b * BLOCK : (b + 1) * BLOCK] = gath[:, b, :]

    lo_op = level_operator(mdiff[...])
    l2 = dot_exact(lo_op[0:8], lo_op)
    width = y_out.shape[0]
    top = []
    cols = iota((1, width), 1)
    for f in range(3):
        n_l = levels_o
        place = (iota((n_l, width), 1) == iota((n_l, width), 0) + f * n_l).astype(F32)
        row = dot_exact(l2, place)[0:1]
        row = row + jnp.where(cols == rows_o + f, lo_op[0:1, 0:1], F32(0.0))
        top.append(row + jnp.where(cols == rows_o + 3 + f, F32(1.0), F32(0.0)))
    top = jnp.concatenate(top + [jnp.zeros((5, width), F32)], axis=0)
    thi = top.astype(BF16).astype(F32)
    tstack = jnp.concatenate([thi, top - thi], axis=0).astype(BF16)
    nt = (((1,), (1,)), ((), ()))
    for b in range(ob):
        yhi, ylo = pieces_of(y_out[:, b * BLOCK : (b + 1) * BLOCK])
        first = dot(tstack, yhi)
        second = dot(tstack, ylo)
        surf = first[0:8] + first[8:16] + second[0:8]
        row_ids = iota((8, BLOCK), 0)
        surf = jnp.where(row_ids == 3, px[FAR, 12, b : b + 1, :], surf)
        shi = surf.astype(BF16).astype(F32)
        sstack = jnp.concatenate([shi, surf - shi], axis=0).astype(BF16)
        first = lax.dot_general(sstack, whi[b], nt, preferred_element_type=F32)
        second = lax.dot_general(sstack, wlo[b], nt, preferred_element_type=F32)
        piece = first[0:8] + first[8:16] + second[0:8]
        for r in range(refs):
            pc[:, b * refs + r, :] = piece[0:4, r * BLOCK : (r + 1) * BLOCK]
    count = ob * refs
    hits = (iota((3 * ab, count), 0) == places[0:1, 0:count]).astype(F32)
    for f in range(4):
        coll[f] = dot_exact(hits, pc[f])
    back_sends = [
        remote(coll.at[:, 2 * ab : 3 * ab, :], rb.at[0], 20, 1),
        remote(coll.at[:, 0:ab, :], rb.at[1], 21, -1),
    ]
    for c in back_sends:
        c.start()

    for s in range(slots):
        coef[s, 7] = 0.1 * ofx[s, 1] * px[s, 12]

    def barotropic(reach):
        def step(i, carry):
            fresh = []
            for s in range(FAR - reach, FAR + reach + 1):
                r = 8 + s * ob
                fresh.append(
                    coef[s, 7]
                    + neighbours(
                        eta[r - 1 : r - 1 + ob, :], eta[r : r + ob, :], eta[r + 1 : r + 1 + ob, :], s
                    )
                )
            for s, value in zip(range(FAR - reach, FAR + reach + 1), fresh):
                eta[8 + s * ob : 8 + (s + 1) * ob, :] = value
            return carry

        return step

    steps = BT_SUB * BC_SUB
    left_over = steps
    for reach in range(FAR, -1, -1):
        stop = max((reach - 1) * ob, -1) if reach else -1
        todo = left_over - 1 - stop
        if reach == FAR:
            todo = left_over - 1 - stop
        lax.fori_loop(0, todo, barotropic(reach), 0)
        left_over -= todo
    ssh_out[...] = eta[8 + FAR * ob : 8 + (FAR + 1) * ob, :]

    pad = jnp.zeros((rows_a - 3 * levels_a, 2 * BLOCK), F32)

    def put_air(value, at, buf):
        rows = jnp.concatenate([value.reshape(3 * levels_a, 2 * BLOCK), pad], axis=0)
        hi, lo = pieces_of(rows)
        buf[0:rows_a, at] = hi
        buf[rows_a : 2 * rows_a, at] = lo

    edge_a = jnp.zeros((2 * rows_a, BLOCK), BF16)
    for buf in (hla, hlb):
        buf[:, 0:BLOCK] = edge_a
        buf[:, buf.shape[1] - BLOCK : buf.shape[1]] = edge_a
    air_copy.wait()

    def fill(j, carry):
        cols = pl.ds(pl.multiple_of(j * 2 * BLOCK, BLOCK), 2 * BLOCK)
        put_air(
            centre[:, :, cols],
            pl.ds(pl.multiple_of(j * 2 * BLOCK + BLOCK + HA, BLOCK), 2 * BLOCK),
            hla,
        )
        return carry

    lax.fori_loop(0, ab // 2, fill, 0)
    for c in list_sends + air_sends:
        c.wait_recv()
    lx[:, 0:HA] = lleft[...]
    lx[:, HA + na : 2 * HA + na] = lright[...]
    lax.fori_loop(0, half, build_air, 0)
    lax.fori_loop(pairs - half, pairs, build_air, 0)
    for j in range(half):
        cols = slice(j * 2 * BLOCK, (j + 1) * 2 * BLOCK)
        base = BLOCK + j * 2 * BLOCK
        put_air(left[:, :, cols], slice(base, base + 2 * BLOCK), hla)
        base = base + HA + na
        put_air(right[:, :, cols], slice(base, base + 2 * BLOCK), hla)

    def air_apply(j, src):
        window = src[:, pl.ds(pl.multiple_of(j * 2 * BLOCK, BLOCK), 4 * BLOCK)]
        r = dot(window, op[j])
        own = src[:, pl.ds(pl.multiple_of(j * 2 * BLOCK + BLOCK, BLOCK), 2 * BLOCK)].astype(F32)
        own = own[0:rows_a] + own[rows_a : 2 * rows_a]
        gain = 1.0 - 0.22 * alist.shape[0]
        return gain * own + 0.22 * (r[0:rows_a] + r[rows_a : 2 * rows_a])

    def air_step(src, dst):
        def step(j, carry):
            hi, lo = pieces_of(air_apply(j, src))
            cols = pl.ds(pl.multiple_of(j * 2 * BLOCK + BLOCK, BLOCK), 2 * BLOCK)
            dst[0:rows_a, cols] = hi
            dst[rows_a : 2 * rows_a, cols] = lo
            return carry

        return step

    lax.fori_loop(0, pairs, air_step(hla, hlb), 0)
    lax.fori_loop(1, pairs - 1, air_step(hlb, hla), 0)
    lax.fori_loop(1, pairs - 1, air_step(hla, hlb), 0)

    def air_last(j, carry):
        cols = pl.ds(pl.multiple_of((j - half) * 2 * BLOCK, BLOCK), 2 * BLOCK)
        t_out[:, cols] = air_apply(j, hlb)
        return carry

    lax.fori_loop(half, pairs - half, air_last, 0)

    for c in back_sends:
        c.wait_recv()
    tot_out[...] = coll[:, ab : 2 * ab, :] + rb[0] + rb[1]
    for c in flux_sends + table_sends + list_sends + mar_sends + air_sends + of_sends + back_sends:
        c.wait_send()


def last_kernel(t, y, tot, ssh, warm, adiff, mdiff, a_out, o_out, skin, ssh_out, mix_a, mix_o):
    rows_a = t.shape[0]
    rows_o = y.shape[0]
    la = adiff.shape[0]
    lo = mdiff.shape[0]
    one = level_operator(adiff[...])
    two = dot_exact(one, one)
    four = dot_exact(two, two)
    oc = level_operator(mdiff[...])
    oc2 = dot_exact(oc, oc)
    at = iota((lo, rows_o), 1)
    level = iota((lo, rows_o), 0)
    for f in range(3):
        m = spread_columns(four, f, rows_a)
        mix_a[f * la : (f + 1) * la, :] = m
        m = spread_columns(oc2, f, rows_o)
        m = m + jnp.where(at == 3 * lo + f, oc[:, 0:1], F32(0.0))
        m = m + jnp.where((at == 3 * lo + 3 + f) & (level == 0), F32(1.0), F32(0.0))
        mix_o[f * lo : (f + 1) * lo, :] = m

    def mix(src, mixer, out, levels):
        mhi, mlo = pieces_of(mixer[...])

        def step(j, carry):
            cols = pl.ds(pl.multiple_of(j * 2 * BLOCK, BLOCK), 2 * BLOCK)
            hi, lo_ = pieces_of(src[:, cols])
            r = dot(mhi, hi) + dot(mlo, hi) + dot(mhi, lo_)
            out[:, :, cols] = r.reshape(3, levels, 2 * BLOCK)
            return carry

        lax.fori_loop(0, src.shape[1] // (2 * BLOCK), step, 0)

    mix(t, mix_a, a_out, la)
    mix(y, mix_o, o_out, lo)
    share = 1.0 + tot[3]
    parts = [(warm[...] + tot[0]) / share, tot[1] / share, tot[2] / share]
    for f in range(3):
        for b in range(tot.shape[1]):
            skin[f : f + 1, b * BLOCK : (b + 1) * BLOCK] = parts[f][b : b + 1, :]
    ssh_out[...] = ssh[...]


def body(
    air, warm, alist, adiff, mar, sea, mlist, mff, mind, mdiff, donor, weights
):
    n = lax.axis_size("col")
    na = air.shape[2]
    no = mar.shape[2]
    ab = na // BLOCK
    ob = no // BLOCK
    la = air.shape[1]
    lo = mar.shape[1]
    refs = donor.shape[1]
    rows_a = -(-3 * la // 16) * 16
    rows_o = 3 * lo
    slots = 2 * FAR + 1
    pairs = ab // 2 + SUB_A
    opairs = ob // 2 + BC_SUB
    wide_a = na + 2 * HA + 2 * BLOCK
    wide_o = no + 2 * HO + 2 * BLOCK
    vmem = pl.BlockSpec(memory_space=pltpu.VMEM)
    anywhere = pl.BlockSpec(memory_space=pl.ANY)
    smem = pl.BlockSpec(memory_space=pltpu.SMEM)
    S = jax.ShapeDtypeStruct
    V = pltpu.VMEM
    t, y, tot, ssh = pl.pallas_call(
        functools.partial(main_kernel, n),
        out_shape=(
            S((rows_a, na), F32), S((rows_o + 16, no), F32), S((4, ab, BLOCK), F32), S((ob, BLOCK), F32),
        ),
        in_specs=[anywhere, vmem, vmem, anywhere, vmem, vmem, vmem, vmem, vmem, smem, anywhere],
        out_specs=(vmem, vmem, vmem, vmem),
        scratch_shapes=[
            V((3, 8, na), F32),
            V((3, la, na), F32), V((3, la, HA), F32), V((3, la, HA), F32),
            V((3, lo, no), F32), V((3, lo, HO), F32), V((3, lo, HO), F32),
            V((4, na + 2 * HA), jnp.int32), V((4, HA), jnp.int32), V((4, HA), jnp.int32),
            V((ob, refs * BLOCK, BLOCK), F32),
            V((ob, refs * BLOCK, BLOCK), BF16), V((ob, refs * BLOCK, BLOCK), BF16),
            V((3 * ab, 4, BLOCK), F32),
            V((slots, 14, ob, BLOCK), F32),
            V((slots, 4, ob, BLOCK), F32),
            V((slots, 6, ob, BLOCK), jnp.int32), V((slots, 8, ob, BLOCK), F32),
            V((slots * ob + 16, BLOCK), F32),
            V((3 * ob, BLOCK), F32),
            V((16, ob, BLOCK), F32),
            V((pairs, 4 * BLOCK, 2 * BLOCK), BF16),
            V((opairs, 4 * BLOCK, 2 * BLOCK), BF16), V((opairs, 4 * BLOCK, 2 * BLOCK), BF16),
            V((2 * rows_a, wide_a), BF16), V((2 * rows_a, wide_a), BF16),
            V((2 * rows_o, wide_o), BF16), V((2 * rows_o, wide_o), BF16),
            V((4, ob * refs, BLOCK), F32), V((4, 3 * ab, BLOCK), F32), V((2, 4, ab, BLOCK), F32),
            pltpu.SemaphoreType.DMA((22,)), pltpu.SemaphoreType.DMA((22,)), pltpu.SemaphoreType.DMA((4,)),
        ],
        compiler_params=pltpu.CompilerParams(
            collective_id=0, has_side_effects=True, vmem_limit_bytes=50 * 1024 * 1024
        ),
        name="couple",
    )(
        air, warm.reshape(1, na), alist, mar, sea.reshape(ob, BLOCK), mlist, mff,
        mind.reshape(ob, BLOCK), mdiff, donor.T, weights.reshape(ob, refs * BLOCK, BLOCK),
    )
    a_out, o_out, skin, ssh_out = pl.pallas_call(
        last_kernel,
        out_shape=(S(air.shape, F32), S(mar.shape, F32), S((3, na), F32), S((ob, BLOCK), F32)),
        in_specs=[vmem] * 7,
        out_specs=(vmem,) * 4,
        scratch_shapes=[V((3 * la, rows_a), F32), V((3 * lo, rows_o + 16), F32)],
        compiler_params=pltpu.CompilerParams(vmem_limit_bytes=50 * 1024 * 1024),
        name="mix",
    )(t, y, tot, ssh, warm.reshape(ab, BLOCK), adiff, mdiff)
    return a_out, o_out, ssh_out.reshape(no), skin


def solution(mesh):
    cells = ("member", "col")
    in_specs = (
        P(None, None, cells),
        P(cells),
        P(None, "col"),
        P(),
        P(None, None, cells),
        P(cells),
        P(None, "col"),
        P(None, "col"),
        P("col"),
        P(),
        P(),
        P("col", None, None, None),
    )
    out_specs = (P(None, None, cells), P(None, None, cells), P(cells), P(None, cells))
    return jax.shard_map(body, mesh=mesh, in_specs=in_specs, out_specs=out_specs, check_vma=False)
```

time: 376 us -> 67.4 us (0.18)
  the two profiles are of different devices: /device:TPU:0 before, /device:TPU:1 now
where the time goes in v1:
time: 67.4 us; the launch traced here: 66.4 us
  Pallas kernels  55.8 us (83%)
  local copies, waits for them, and re-layouts  9.97 us (15%)
  between operations  0.69 us (1%)
    pallas_call x1, Pallas kernels, body(): pl.pallas_call(functools.partial(main_kernel, n), out_shape=(S((rows_a, n...  50.4 us
    unnamed x26, local copies, waits for them, and re-layouts  9.97 us
    pallas_call x1, Pallas kernels, body(): pl.pallas_call(last_kernel, out_shape=(S(air.shape, F32), S(mar.shape, F3...  5.37 us

profile of v1, /device:TPU:1, one launch (start us, length us, event | category | flops | bytes accessed | tf_op | source)
XLA Modules:
  0.0 66.4 jit_solution(14525568402051076889)
XLA Ops:
  0.6 0.0 copy-start.1
  0.6 1.5 %copy-done.1 = f32[3,72,2048]{2,1,0:T(8,128)S(1)} copy-done((f32[3,72,2048]{2,1,0:T(8,128)S(1)}, f32[3,72,2048]{2,1,0:T(8,128)}, u32[]{:S(2)}) %copy-start.1) | copy-done | bytes 1769496
  2.1 0.0 copy-start.2
  2.1 1.2 %copy-done.2 = f32[3,80,1024]{2,1,0:T(8,128)S(1)} copy-done((f32[3,80,1024]{2,1,0:T(8,128)S(1)}, f32[3,80,1024]{2,1,0:T(8,128)}, u32[]{:S(2)}) %copy-start.2) | copy-done | bytes 983064
  3.3 0.0 copy-start.3
  3.3 0.8 %copy-done.3 = f32[80,80]{1,0:T(8,128)S(1)} copy-done((f32[80,80]{1,0:T(8,128)S(1)}, f32[80,80]{1,0:T(8,128)}, u32[]{:S(2)}) %copy-start.3) | copy-done | bytes 25624
  4.1 0.0 copy-start.5
  4.1 0.8 %copy-done.5 = s32[4,2048]{1,0:T(4,128)S(1)} copy-done((s32[4,2048]{1,0:T(4,128)S(1)}, s32[4,2048]{1,0:T(4,128)}, u32[]{:S(2)}) %copy-start.5) | copy-done | bytes 32792
  4.9 0.0 copy-start.6
  4.9 0.8 %copy-done.6 = s32[6,1024]{1,0:T(8,128)S(1)} copy-done((s32[6,1024]{1,0:T(8,128)S(1)}, s32[6,1024]{1,0:T(8,128)}, u32[]{:S(2)}) %copy-start.6) | copy-done | bytes 24600
  5.6 0.0 copy-start.7
  5.6 0.8 %copy-done.7 = f32[6,1024]{1,0:T(8,128)S(1)} copy-done((f32[6,1024]{1,0:T(8,128)S(1)}, f32[6,1024]{1,0:T(8,128)}, u32[]{:S(2)}) %copy-start.7) | copy-done | bytes 24600
  6.4 0.0 copy-start.8
  6.4 0.7 %copy-done.8 = f32[2048]{0:T(1024)S(1)} copy-done((f32[2048]{0:T(1024)S(1)}, f32[2048]{0:T(1024)}, u32[]{:S(2)}) %copy-start.8) | copy-done | bytes 8216
  7.1 0.0 copy-start.10
  7.1 0.7 %copy-done.10 = f32[1024]{0:T(1024)S(1)} copy-done((f32[1024]{0:T(1024)S(1)}, f32[1024]{0:T(1024)}, u32[]{:S(2)}) %copy-start.10) | copy-done | bytes 4120
  7.8 0.0 copy-start.11
  7.8 0.7 %copy-done.11 = s32[1024]{0:T(1024)S(1)} copy-done((s32[1024]{0:T(1024)S(1)}, s32[1024]{0:T(1024)}, u32[]{:S(2)}) %copy-start.11) | copy-done | bytes 4120
  8.4 0.0 copy-start.12
  8.4 0.7 %copy-done.12 = s32[128,4]{0,1:T(4,128)S(1)} copy-done((s32[128,4]{0,1:T(4,128)S(1)}, s32[128,4]{0,1:T(4,128)}, u32[]{:S(2)}) %copy-start.12) | copy-done | bytes 2072
  9.1 0.0 copy-start.4
  9.1 0.0 copy-start.9
  9.1 50.4 %couple.1 = (f32[224,2048]{1,0:T(8,128)}, f32[256,1024]{1,0:T(8,128)S(1)}, f32[4,16,128]{2,1,0:T(8,128)S(1)}, f32[8,128]{1,0:T(8,128)S(1)}) custom-call(f32[3,72,2048]{2,1,0:T(8,128)S(1)} %copy-done.1, f32[1,2048]{1,0:T(1,128)S(1)} %bitcast.7, s32[4,2048]{1,0:T(4,128)S(1)} %copy-done.5, f32[3,80,1024]{2,1,0:T(8,128)S(1)} %copy-done.2, f32[8,128]{1,0:T(8,128)S(1)} %bitcast.9, ...), custom_call_target="tpu_custom_call" | custom-call | tf_op jit(solution)/shard_map/couple/pallas_call | solution.py:530
  59.5 0.0 copy-done.4
  59.5 0.0 copy-done.9
  59.6 0.0 copy-start
  59.6 1.5 %copy-done = f32[224,2048]{1,0:T(8,128)S(1)} copy-done((f32[224,2048]{1,0:T(8,128)S(1)}, f32[224,2048]{1,0:T(8,128)}, u32[]{:S(2)}) %copy-start) | copy-done | bytes 1835032
  61.1 5.4 %mix.1 = (f32[3,72,2048]{2,1,0:T(8,128)}, f32[3,80,1024]{2,1,0:T(8,128)}, f32[3,2048]{1,0:T(4,128)}, f32[8,128]{1,0:T(8,128)}) custom-call(f32[224,2048]{1,0:T(8,128)S(1)} %copy-done, f32[256,1024]{1,0:T(8,128)S(1)} %get-tuple-element.13.y, f32[4,16,128]{2,1,0:T(8,128)S(1)} %get-tuple-element.14.tot, f32[8,128]{1,0:T(8,128)S(1)} %get-tuple-element.15.ssh, ...), custom_call_target="tpu_custom_call" | custom-call | tf_op jit(solution)/shard_map/mix/pallas_call | solution.py:566
Async XLA Ops:
  0.6 1.5 %copy-start.1 = (f32[3,72,2048]{2,1,0:T(8,128)S(1)}, f32[3,72,2048]{2,1,0:T(8,128)}, u32[]{:S(2)}) copy-start(f32[3,72,2048]{2,1,0:T(8,128)} %air.1) | copy-start | bytes 5308420
  2.1 1.2 %copy-start.2 = (f32[3,80,1024]{2,1,0:T(8,128)S(1)}, f32[3,80,1024]{2,1,0:T(8,128)}, u32[]{:S(2)}) copy-start(f32[3,80,1024]{2,1,0:T(8,128)} %mar.1) | copy-start | bytes 2949124
  3.3 0.8 %copy-start.3 = (f32[80,80]{1,0:T(8,128)S(1)}, f32[80,80]{1,0:T(8,128)}, u32[]{:S(2)}) copy-start(f32[80,80]{1,0:T(8,128)} %mdiff.3) | copy-start | bytes 76804
  4.1 0.8 %copy-start.5 = (s32[4,2048]{1,0:T(4,128)S(1)}, s32[4,2048]{1,0:T(4,128)}, u32[]{:S(2)}) copy-start(s32[4,2048]{1,0:T(4,128)} %alist.1) | copy-start | bytes 98308
  4.9 0.8 %copy-start.6 = (s32[6,1024]{1,0:T(8,128)S(1)}, s32[6,1024]{1,0:T(8,128)}, u32[]{:S(2)}) copy-start(s32[6,1024]{1,0:T(8,128)} %mlist.1) | copy-start | bytes 73732
  5.6 0.8 %copy-start.7 = (f32[6,1024]{1,0:T(8,128)S(1)}, f32[6,1024]{1,0:T(8,128)}, u32[]{:S(2)}) copy-start(f32[6,1024]{1,0:T(8,128)} %mff.1) | copy-start | bytes 73732
  6.4 0.7 %copy-start.8 = (f32[2048]{0:T(1024)S(1)}, f32[2048]{0:T(1024)}, u32[]{:S(2)}) copy-start(f32[2048]{0:T(1024)} %param.13) | copy-start | bytes 24580
  7.1 0.7 %copy-start.10 = (f32[1024]{0:T(1024)S(1)}, f32[1024]{0:T(1024)}, u32[]{:S(2)}) copy-start(f32[1024]{0:T(1024)} %param.17) | copy-start | bytes 12292
  7.8 0.7 %copy-start.11 = (s32[1024]{0:T(1024)S(1)}, s32[1024]{0:T(1024)}, u32[]{:S(2)}) copy-start(s32[1024]{0:T(1024)} %param.20) | copy-start | bytes 12292
  8.4 0.7 %copy-start.12 = (s32[128,4]{0,1:T(4,128)S(1)}, s32[128,4]{0,1:T(4,128)}, u32[]{:S(2)}) copy-start(s32[128,4]{0,1:T(4,128)} %param.22) | copy-start | bytes 6148
  9.1 50.4 %copy-start.4 = (f32[72,72]{1,0:T(8,128)S(1)}, f32[72,72]{1,0:T(8,128)}, u32[]{:S(2)}) copy-start(f32[72,72]{1,0:T(8,128)} %adiff.1) | copy-start | bytes 62212
  9.1 50.4 %copy-start.9 = (f32[2048]{0:T(1024)S(1)}, f32[2048]{0:T(1024)}, u32[]{:S(2)}) copy-start(f32[2048]{0:T(1024)} %param.13) | copy-start | bytes 24580
  59.6 1.5 %copy-start = (f32[224,2048]{1,0:T(8,128)S(1)}, f32[224,2048]{1,0:T(8,128)}, u32[]{:S(2)}) copy-start(f32[224,2048]{1,0:T(8,128)} %get-tuple-element.12.t) | copy-start | bytes 5505028

commit v2 on v1

--- a/solution.py
+++ b/solution.py
@@ -15,7 +15,8 @@
 F32 = jnp.float32
 BF16 = jnp.bfloat16
 HIGHEST = lax.Precision.HIGHEST
-FAR = 3
+FAR = 1
+ROUNDS = (7, 7, 6)
 HA = SUB_A * BLOCK
 HO = BC_SUB * BLOCK
 
@@ -54,11 +55,12 @@
 
 def main_kernel(
     n,
-    air, warm, alist, mar, sea, mlist, mff, mind, mdiff, donor, weights,
+    air, warm_in, alist_in, mar, sea_in, mlist_in, mff_in, mind_in, mdiff_in, donor_in, weights,
     t_out, y_out, tot_out, ssh_out,
+    warm, alist, sea, mlist, mff, mind, mdiff, donor,
     low, centre, left, right, xc, xl, xr, lx, lleft, lright,
     wf, whi, wlo, cand, px, ofx, idx, coef, eta, forc, gath, op, fhi, flo,
-    hla, hlb, xa, xb, pc, coll, rb,
+    hla, hlb, xa, xb, pc, coll, rb, es, el, er,
     ss, rs, ls,
 ):
     levels_a = air.shape[1]
@@ -69,7 +71,7 @@
     ob = no // BLOCK
     rows_a = hla.shape[0] // 2
     rows_o = xa.shape[0] // 2
-    refs = donor.shape[0]
+    refs = donor_in.shape[0]
     me = lax.axis_index("col")
 
     def peer(d):
@@ -83,6 +85,17 @@
 
     low_copy = pltpu.make_async_copy(air.at[:, levels_a - 8 :, :], low, ls.at[0])
     low_copy.start()
+    small = [
+        pltpu.make_async_copy(a, b, ls.at[4 + i])
+        for i, (a, b) in enumerate(
+            [
+                (mlist_in, mlist), (mff_in, mff), (mind_in, mind), (sea_in, sea),
+                (warm_in, warm), (alist_in, alist), (donor_in, donor), (mdiff_in, mdiff),
+            ]
+        )
+    ]
+    for c in small:
+        c.start()
     w_copy = pltpu.make_async_copy(weights, wf, ls.at[1])
     air_copy = pltpu.make_async_copy(air, centre, ls.at[2])
     mar_copy = pltpu.make_async_copy(mar, xc, ls.at[3])
@@ -93,6 +106,9 @@
     barrier = pltpu.get_barrier_semaphore()
     for d in far:
         pl.semaphore_signal(barrier, inc=1, device_id=peer(d), device_id_type=MESH)
+
+    for c in small:
+        c.wait()
 
     for b in range(ob):
         cols = slice(b * BLOCK, (b + 1) * BLOCK)
@@ -246,6 +262,66 @@
 
     lax.fori_loop(0, opairs, build_ocean, 0)
 
+    for c in of_sends:
+        c.wait_recv()
+
+    def neighbours(prev, cur, after, s):
+        total = coef[s, 6] * cur
+        for k in range(6):
+            at = idx[s, k]
+            lanes = jnp.bitwise_and(at, BLOCK - 1)
+            g0 = gather_lanes(prev, lanes)
+            g1 = gather_lanes(cur, lanes)
+            g2 = gather_lanes(after, lanes)
+            g = jnp.where(at < BLOCK, g0, jnp.where(at < 2 * BLOCK, g1, g2))
+            total = total + coef[s, k] * g
+        return total
+
+    for s in range(slots):
+        coef[s, 7] = 0.1 * ofx[s, 1] * px[s, 12]
+
+    own_rows = slice(8 + FAR * ob, 8 + (FAR + 1) * ob)
+
+    def barotropic(reach):
+        def step(i, carry):
+            fresh = []
+            for s in range(FAR - reach, FAR + reach + 1):
+                r = 8 + s * ob
+                fresh.append(
+                    coef[s, 7]
+                    + neighbours(
+                        eta[r - 1 : r - 1 + ob, :], eta[r : r + ob, :], eta[r + 1 : r + 1 + ob, :], s
+                    )
+                )
+            for s, value in zip(range(FAR - reach, FAR + reach + 1), fresh):
+                eta[8 + s * ob : 8 + (s + 1) * ob, :] = value
+            return carry
+
+        return step
+
+    def eta_round(i):
+        if i > 0:
+            for c in eta_sends[-2:]:
+                c.wait_recv()
+            eta[8 : 8 + ob, :] = el[i - 1]
+            eta[8 + (FAR + 1) * ob : 8 + (FAR + 2) * ob, :] = er[i - 1]
+        lax.fori_loop(0, ROUNDS[i] - 1, barotropic(1), 0)
+        barotropic(0)(0, 0)
+        if i + 1 < len(ROUNDS):
+            es[i] = eta[own_rows, :]
+            pair = [
+                remote(es.at[i], el.at[i], 22 + 2 * i, 1),
+                remote(es.at[i], er.at[i], 23 + 2 * i, -1),
+            ]
+            for c in pair:
+                c.start()
+            eta_sends.extend(pair)
+        else:
+            ssh_out[...] = eta[own_rows, :]
+
+    eta_sends = []
+    eta_round(0)
+
     def put_ocean(value, at, buf):
         rows = value.reshape(rows_o, value.shape[2])
         hi, lo = pieces_of(rows)
@@ -290,21 +366,6 @@
         return carry
 
     lax.fori_loop(1, opairs - 1, ocean_second, 0)
-
-    for c in of_sends:
-        c.wait_recv()
-
-    def neighbours(prev, cur, after, s):
-        total = coef[s, 6] * cur
-        for k in range(6):
-            at = idx[s, k]
-            lanes = jnp.bitwise_and(at, BLOCK - 1)
-            g0 = gather_lanes(prev, lanes)
-            g1 = gather_lanes(cur, lanes)
-            g2 = gather_lanes(after, lanes)
-            g = jnp.where(at < BLOCK, g0, jnp.where(at < 2 * BLOCK, g1, g2))
-            total = total + coef[s, k] * g
-        return total
 
     gath[...] = jnp.zeros(gath.shape, F32)
     for i, field in enumerate((0, 2, 3)):
@@ -358,36 +419,7 @@
     for c in back_sends:
         c.start()
 
-    for s in range(slots):
-        coef[s, 7] = 0.1 * ofx[s, 1] * px[s, 12]
-
-    def barotropic(reach):
-        def step(i, carry):
-            fresh = []
-            for s in range(FAR - reach, FAR + reach + 1):
-                r = 8 + s * ob
-                fresh.append(
-                    coef[s, 7]
-                    + neighbours(
-                        eta[r - 1 : r - 1 + ob, :], eta[r : r + ob, :], eta[r + 1 : r + 1 + ob, :], s
-                    )
-                )
-            for s, value in zip(range(FAR - reach, FAR + reach + 1), fresh):
-                eta[8 + s * ob : 8 + (s + 1) * ob, :] = value
-            return carry
-
-        return step
-
-    steps = BT_SUB * BC_SUB
-    left_over = steps
-    for reach in range(FAR, -1, -1):
-        stop = max((reach - 1) * ob, -1) if reach else -1
-        todo = left_over - 1 - stop
-        if reach == FAR:
-            todo = left_over - 1 - stop
-        lax.fori_loop(0, todo, barotropic(reach), 0)
-        left_over -= todo
-    ssh_out[...] = eta[8 + FAR * ob : 8 + (FAR + 1) * ob, :]
+    eta_round(1)
 
     pad = jnp.zeros((rows_a - 3 * levels_a, 2 * BLOCK), F32)
 
@@ -413,6 +445,29 @@
         return carry
 
     lax.fori_loop(0, ab // 2, fill, 0)
+    def air_apply(j, src):
+        window = src[:, pl.ds(pl.multiple_of(j * 2 * BLOCK, BLOCK), 4 * BLOCK)]
+        r = dot(window, op[j])
+        own = src[:, pl.ds(pl.multiple_of(j * 2 * BLOCK + BLOCK, BLOCK), 2 * BLOCK)].astype(F32)
+        own = own[0:rows_a] + own[rows_a : 2 * rows_a]
+        gain = 1.0 - 0.22 * alist.shape[0]
+        return gain * own + 0.22 * (r[0:rows_a] + r[rows_a : 2 * rows_a])
+
+    def air_step(src, dst):
+        def step(j, carry):
+            hi, lo = pieces_of(air_apply(j, src))
+            cols = pl.ds(pl.multiple_of(j * 2 * BLOCK + BLOCK, BLOCK), 2 * BLOCK)
+            dst[0:rows_a, cols] = hi
+            dst[rows_a : 2 * rows_a, cols] = lo
+            return carry
+
+        return step
+
+    inner = half + 1
+    lax.fori_loop(inner, pairs - inner, air_step(hla, hlb), 0)
+    lax.fori_loop(inner + 1, pairs - inner - 1, air_step(hlb, hla), 0)
+    eta_round(2)
+
     for c in list_sends + air_sends:
         c.wait_recv()
     lx[:, 0:HA] = lleft[...]
@@ -426,26 +481,10 @@
         base = base + HA + na
         put_air(right[:, :, cols], slice(base, base + 2 * BLOCK), hla)
 
-    def air_apply(j, src):
-        window = src[:, pl.ds(pl.multiple_of(j * 2 * BLOCK, BLOCK), 4 * BLOCK)]
-        r = dot(window, op[j])
-        own = src[:, pl.ds(pl.multiple_of(j * 2 * BLOCK + BLOCK, BLOCK), 2 * BLOCK)].astype(F32)
-        own = own[0:rows_a] + own[rows_a : 2 * rows_a]
-        gain = 1.0 - 0.22 * alist.shape[0]
-        return gain * own + 0.22 * (r[0:rows_a] + r[rows_a : 2 * rows_a])
-
-    def air_step(src, dst):
-        def step(j, carry):
-            hi, lo = pieces_of(air_apply(j, src))
-            cols = pl.ds(pl.multiple_of(j * 2 * BLOCK + BLOCK, BLOCK), 2 * BLOCK)
-            dst[0:rows_a, cols] = hi
-            dst[rows_a : 2 * rows_a, cols] = lo
-            return carry
-
-        return step
-
-    lax.fori_loop(0, pairs, air_step(hla, hlb), 0)
-    lax.fori_loop(1, pairs - 1, air_step(hlb, hla), 0)
+    lax.fori_loop(0, inner, air_step(hla, hlb), 0)
+    lax.fori_loop(pairs - inner, pairs, air_step(hla, hlb), 0)
+    lax.fori_loop(1, inner + 1, air_step(hlb, hla), 0)
+    lax.fori_loop(pairs - inner - 1, pairs - 1, air_step(hlb, hla), 0)
     lax.fori_loop(1, pairs - 1, air_step(hla, hlb), 0)
 
     def air_last(j, carry):
@@ -458,11 +497,22 @@
     for c in back_sends:
         c.wait_recv()
     tot_out[...] = coll[:, ab : 2 * ab, :] + rb[0] + rb[1]
-    for c in flux_sends + table_sends + list_sends + mar_sends + air_sends + of_sends + back_sends:
+    for c in flux_sends + table_sends + list_sends + mar_sends + air_sends + of_sends + back_sends + eta_sends:
         c.wait_send()
 
 
-def last_kernel(t, y, tot, ssh, warm, adiff, mdiff, a_out, o_out, skin, ssh_out, mix_a, mix_o):
+def last_kernel(
+    t_in, y_in, tot_in, ssh_in, warm_in, adiff_in, mdiff_in,
+    a_out, o_out, skin, ssh_out,
+    t, y, tot, warm, adiff, mdiff,
+    mix_a, mix_o, a_buf, o_buf, sem, in_sem,
+):
+    moves = [(adiff_in, adiff), (mdiff_in, mdiff), (t_in, t), (y_in, y), (tot_in, tot), (warm_in, warm), (ssh_in, ssh_out)]
+    ins = [pltpu.make_async_copy(a, b, in_sem.at[i]) for i, (a, b) in enumerate(moves)]
+    for c in ins:
+        c.start()
+    ins[0].wait()
+    ins[1].wait()
     rows_a = t.shape[0]
     rows_o = y.shape[0]
     la = adiff.shape[0]
@@ -482,26 +532,32 @@
         m = m + jnp.where((at == 3 * lo + 3 + f) & (level == 0), F32(1.0), F32(0.0))
         mix_o[f * lo : (f + 1) * lo, :] = m
 
-    def mix(src, mixer, out, levels):
+    def mix(src, mixer, buf, out, levels):
         mhi, mlo = pieces_of(mixer[...])
 
-        def step(j, carry):
-            cols = pl.ds(pl.multiple_of(j * 2 * BLOCK, BLOCK), 2 * BLOCK)
+        for j in range(src.shape[1] // (2 * BLOCK)):
+            cols = slice(j * 2 * BLOCK, (j + 1) * 2 * BLOCK)
             hi, lo_ = pieces_of(src[:, cols])
             r = dot(mhi, hi) + dot(mlo, hi) + dot(mhi, lo_)
-            out[:, :, cols] = r.reshape(3, levels, 2 * BLOCK)
-            return carry
-
-        lax.fori_loop(0, src.shape[1] // (2 * BLOCK), step, 0)
-
-    mix(t, mix_a, a_out, la)
-    mix(y, mix_o, o_out, lo)
+            buf[:, :, cols] = r.reshape(3, levels, 2 * BLOCK)
+            copy = pltpu.make_async_copy(buf.at[:, :, cols], out.at[:, :, cols], sem.at[len(copies)])
+            copy.start()
+            copies.append(copy)
+
+    copies = []
+    ins[2].wait()
+    mix(t, mix_a, a_buf, a_out, la)
+    ins[3].wait()
+    mix(y, mix_o, o_buf, o_out, lo)
+    for c in ins[4:]:
+        c.wait()
     share = 1.0 + tot[3]
     parts = [(warm[...] + tot[0]) / share, tot[1] / share, tot[2] / share]
     for f in range(3):
         for b in range(tot.shape[1]):
             skin[f : f + 1, b * BLOCK : (b + 1) * BLOCK] = parts[f][b : b + 1, :]
-    ssh_out[...] = ssh[...]
+    for copy in copies:
+        copy.wait()
 
 
 def body(
@@ -523,8 +579,7 @@
     wide_a = na + 2 * HA + 2 * BLOCK
     wide_o = no + 2 * HO + 2 * BLOCK
     vmem = pl.BlockSpec(memory_space=pltpu.VMEM)
-    anywhere = pl.BlockSpec(memory_space=pl.ANY)
-    smem = pl.BlockSpec(memory_space=pltpu.SMEM)
+    hbm = pl.BlockSpec(memory_space=pl.ANY)
     S = jax.ShapeDtypeStruct
     V = pltpu.VMEM
     t, y, tot, ssh = pl.pallas_call(
@@ -532,9 +587,12 @@
         out_shape=(
             S((rows_a, na), F32), S((rows_o + 16, no), F32), S((4, ab, BLOCK), F32), S((ob, BLOCK), F32),
         ),
-        in_specs=[anywhere, vmem, vmem, anywhere, vmem, vmem, vmem, vmem, vmem, smem, anywhere],
+        in_specs=[hbm] * 11,
         out_specs=(vmem, vmem, vmem, vmem),
         scratch_shapes=[
+            V((1, na), F32), V(alist.shape, jnp.int32), V((ob, BLOCK), F32), V(mlist.shape, jnp.int32),
+            V(mff.shape, F32), V((ob, BLOCK), jnp.int32), V(mdiff.shape, F32),
+            pltpu.SMEM((refs, donor.shape[0]), jnp.int32),
             V((3, 8, na), F32),
             V((3, la, na), F32), V((3, la, HA), F32), V((3, la, HA), F32),
             V((3, lo, no), F32), V((3, lo, HO), F32), V((3, lo, HO), F32),
@@ -553,10 +611,11 @@
             V((2 * rows_a, wide_a), BF16), V((2 * rows_a, wide_a), BF16),
             V((2 * rows_o, wide_o), BF16), V((2 * rows_o, wide_o), BF16),
             V((4, ob * refs, BLOCK), F32), V((4, 3 * ab, BLOCK), F32), V((2, 4, ab, BLOCK), F32),
-            pltpu.SemaphoreType.DMA((22,)), pltpu.SemaphoreType.DMA((22,)), pltpu.SemaphoreType.DMA((4,)),
+            V((2, ob, BLOCK), F32), V((2, ob, BLOCK), F32), V((2, ob, BLOCK), F32),
+            pltpu.SemaphoreType.DMA((26,)), pltpu.SemaphoreType.DMA((26,)), pltpu.SemaphoreType.DMA((12,)),
         ],
         compiler_params=pltpu.CompilerParams(
-            collective_id=0, has_side_effects=True, vmem_limit_bytes=50 * 1024 * 1024
+            collective_id=0, has_side_effects=True, vmem_limit_bytes=63 * 1024 * 1024
         ),
         name="couple",
     )(
@@ -566,10 +625,16 @@
     a_out, o_out, skin, ssh_out = pl.pallas_call(
         last_kernel,
         out_shape=(S(air.shape, F32), S(mar.shape, F32), S((3, na), F32), S((ob, BLOCK), F32)),
-        in_specs=[vmem] * 7,
-        out_specs=(vmem,) * 4,
-        scratch_shapes=[V((3 * la, rows_a), F32), V((3 * lo, rows_o + 16), F32)],
-        compiler_params=pltpu.CompilerParams(vmem_limit_bytes=50 * 1024 * 1024),
+        in_specs=[hbm] * 7,
+        out_specs=(hbm, hbm, vmem, vmem),
+        scratch_shapes=[
+            V((rows_a, na), F32), V((rows_o + 16, no), F32), V((4, ab, BLOCK), F32), V((ab, BLOCK), F32),
+            V(adiff.shape, F32), V(mdiff.shape, F32),
+            V((3 * la, rows_a), F32), V((3 * lo, rows_o + 16), F32), V(air.shape, F32), V(mar.shape, F32),
+            pltpu.SemaphoreType.DMA(((na + no) // (2 * BLOCK),)),
+            pltpu.SemaphoreType.DMA((7,)),
+        ],
+        compiler_params=pltpu.CompilerParams(vmem_limit_bytes=63 * 1024 * 1024),
         name="mix",
     )(t, y, tot, ssh, warm.reshape(ab, BLOCK), adiff, mdiff)
     return a_out, o_out, ssh_out.reshape(no), skin

time: 67.4 us -> 52.3 us (0.78); the launches traced: 66.4 us -> 52.2 us
  local copies, waits for them, and re-layouts: 9.97 us -> 0 us
  Pallas kernels: 55.8 us -> 51.6 us
    unnamed x26 -> x0, local copies, waits for them, and re-layouts: 9.97 us -> none
    pallas_call x1, Pallas kernels: 50.4 us -> 46.8 us  [body(): pl.pallas_call(functools.partial(main_kernel, n), out_shape=(S((rows_a, n...]
where the time goes in v2:
time: 52.3 us; the launch traced here: 52.2 us
  Pallas kernels  51.6 us (99%)
  between operations  0.64 us (1%)
    pallas_call x1, Pallas kernels, body(): pl.pallas_call(functools.partial(main_kernel, n), out_shape=(S((rows_a, n...  46.8 us
    pallas_call x1, Pallas kernels, body(): pl.pallas_call(last_kernel, out_shape=(S(air.shape, F32), S(mar.shape, F3...  4.76 us

profile of v2, /device:TPU:1, one launch (start us, length us, event | category | flops | bytes accessed | tf_op | source)
XLA Modules:
  0.0 52.2 jit_solution(16204465121986131436)
XLA Ops:
  0.6 46.8 %couple.1 = (f32[224,2048]{1,0:T(8,128)}, f32[256,1024]{1,0:T(8,128)}, f32[4,16,128]{2,1,0:T(8,128)}, f32[8,128]{1,0:T(8,128)}) custom-call(f32[3,72,2048]{2,1,0:T(8,128)} %air.1, f32[1,2048]{1,0:T(1,128)} %bitcast.8, s32[4,2048]{1,0:T(4,128)} %alist_in.1, f32[3,80,1024]{2,1,0:T(8,128)} %mar.1, f32[8,128]{1,0:T(8,128)} %bitcast.10, s32[6,1024]{1,0:T(8,128)} %mlist_in.1, ...), custom_call_target="tpu_custom_call" | custom-call | tf_op jit(solution)/shard_map/couple/pallas_call | solution.py:585
  47.4 4.8 %mix.1 = (f32[3,72,2048]{2,1,0:T(8,128)}, f32[3,80,1024]{2,1,0:T(8,128)}, f32[3,2048]{1,0:T(4,128)}, f32[8,128]{1,0:T(8,128)}) custom-call(f32[224,2048]{1,0:T(8,128)} %get-tuple-element.12.t_in, f32[256,1024]{1,0:T(8,128)} %get-tuple-element.13.y_in, f32[4,16,128]{2,1,0:T(8,128)} %get-tuple-element.14.tot_in, f32[8,128]{1,0:T(8,128)} %get-tuple-element.15.ssh_in, ...), custom_call_target="tpu_custom_call" | custom-call | tf_op jit(solution)/shard_map/mix/pallas_call | solution.py:625

commit v3 on v2

--- a/solution.py
+++ b/solution.py
@@ -186,11 +186,10 @@
     lax.fori_loop(0, ob, split_weights, 0)
 
     def place_of(b, r):
-        ref = donor[r, me * ob + b]
-        owner = ref // ab
-        off = lax.rem(owner - me + n, n)
-        base = jnp.where(off == 0, ab, jnp.where(off == 1, 2 * ab, 0))
-        return base + lax.rem(ref, ab)
+        at = donor[r, me * ob + b] - (me - 1) * ab
+        at = jnp.where(at < 0, at + n * ab, at)
+        at = jnp.where(at >= n * ab, at - n * ab, at)
+        return jnp.minimum(jnp.maximum(at, 0), 3 * ab - 1)
 
     for c in flux_sends:
         c.wait_recv()
@@ -261,6 +260,52 @@
         return carry
 
     lax.fori_loop(0, opairs, build_ocean, 0)
+
+    pad = jnp.zeros((rows_a - 3 * levels_a, 2 * BLOCK), F32)
+
+    def put_air(value, at, buf):
+        rows = jnp.concatenate([value.reshape(3 * levels_a, 2 * BLOCK), pad], axis=0)
+        hi, lo = pieces_of(rows)
+        buf[0:rows_a, at] = hi
+        buf[rows_a : 2 * rows_a, at] = lo
+
+    edge_a = jnp.zeros((2 * rows_a, BLOCK), BF16)
+    for buf in (hla, hlb):
+        buf[:, 0:BLOCK] = edge_a
+        buf[:, buf.shape[1] - BLOCK : buf.shape[1]] = edge_a
+    air_copy.wait()
+
+    def fill(j, carry):
+        cols = pl.ds(pl.multiple_of(j * 2 * BLOCK, BLOCK), 2 * BLOCK)
+        put_air(
+            centre[:, :, cols],
+            pl.ds(pl.multiple_of(j * 2 * BLOCK + BLOCK + HA, BLOCK), 2 * BLOCK),
+            hla,
+        )
+        return carry
+
+    lax.fori_loop(0, ab // 2, fill, 0)
+    def air_apply(j, src):
+        window = src[:, pl.ds(pl.multiple_of(j * 2 * BLOCK, BLOCK), 4 * BLOCK)]
+        r = dot(window, op[j])
+        own = src[:, pl.ds(pl.multiple_of(j * 2 * BLOCK + BLOCK, BLOCK), 2 * BLOCK)].astype(F32)
+        own = own[0:rows_a] + own[rows_a : 2 * rows_a]
+        gain = 1.0 - 0.22 * alist.shape[0]
+        return gain * own + 0.22 * (r[0:rows_a] + r[rows_a : 2 * rows_a])
+
+    def air_step(src, dst):
+        def step(j, carry):
+            hi, lo = pieces_of(air_apply(j, src))
+            cols = pl.ds(pl.multiple_of(j * 2 * BLOCK + BLOCK, BLOCK), 2 * BLOCK)
+            dst[0:rows_a, cols] = hi
+            dst[rows_a : 2 * rows_a, cols] = lo
+            return carry
+
+        return step
+
+    inner = half + 1
+    lax.fori_loop(inner, pairs - inner, air_step(hla, hlb), 0, unroll=2)
+    lax.fori_loop(inner + 1, pairs - inner - 1, air_step(hlb, hla), 0, unroll=2)
 
     for c in of_sends:
         c.wait_recv()
@@ -421,53 +466,6 @@
 
     eta_round(1)
 
-    pad = jnp.zeros((rows_a - 3 * levels_a, 2 * BLOCK), F32)
-
-    def put_air(value, at, buf):
-        rows = jnp.concatenate([value.reshape(3 * levels_a, 2 * BLOCK), pad], axis=0)
-        hi, lo = pieces_of(rows)
-        buf[0:rows_a, at] = hi
-        buf[rows_a : 2 * rows_a, at] = lo
-
-    edge_a = jnp.zeros((2 * rows_a, BLOCK), BF16)
-    for buf in (hla, hlb):
-        buf[:, 0:BLOCK] = edge_a
-        buf[:, buf.shape[1] - BLOCK : buf.shape[1]] = edge_a
-    air_copy.wait()
-
-    def fill(j, carry):
-        cols = pl.ds(pl.multiple_of(j * 2 * BLOCK, BLOCK), 2 * BLOCK)
-        put_air(
-            centre[:, :, cols],
-            pl.ds(pl.multiple_of(j * 2 * BLOCK + BLOCK + HA, BLOCK), 2 * BLOCK),
-            hla,
-        )
-        return carry
-
-    lax.fori_loop(0, ab // 2, fill, 0)
-    def air_apply(j, src):
-        window = src[:, pl.ds(pl.multiple_of(j * 2 * BLOCK, BLOCK), 4 * BLOCK)]
-        r = dot(window, op[j])
-        own = src[:, pl.ds(pl.multiple_of(j * 2 * BLOCK + BLOCK, BLOCK), 2 * BLOCK)].astype(F32)
-        own = own[0:rows_a] + own[rows_a : 2 * rows_a]
-        gain = 1.0 - 0.22 * alist.shape[0]
-        return gain * own + 0.22 * (r[0:rows_a] + r[rows_a : 2 * rows_a])
-
-    def air_step(src, dst):
-        def step(j, carry):
-            hi, lo = pieces_of(air_apply(j, src))
-            cols = pl.ds(pl.multiple_of(j * 2 * BLOCK + BLOCK, BLOCK), 2 * BLOCK)
-            dst[0:rows_a, cols] = hi
-            dst[rows_a : 2 * rows_a, cols] = lo
-            return carry
-
-        return step
-
-    inner = half + 1
-    lax.fori_loop(inner, pairs - inner, air_step(hla, hlb), 0)
-    lax.fori_loop(inner + 1, pairs - inner - 1, air_step(hlb, hla), 0)
-    eta_round(2)
-
     for c in list_sends + air_sends:
         c.wait_recv()
     lx[:, 0:HA] = lleft[...]
@@ -481,18 +479,19 @@
         base = base + HA + na
         put_air(right[:, :, cols], slice(base, base + 2 * BLOCK), hla)
 
-    lax.fori_loop(0, inner, air_step(hla, hlb), 0)
-    lax.fori_loop(pairs - inner, pairs, air_step(hla, hlb), 0)
-    lax.fori_loop(1, inner + 1, air_step(hlb, hla), 0)
-    lax.fori_loop(pairs - inner - 1, pairs - 1, air_step(hlb, hla), 0)
-    lax.fori_loop(1, pairs - 1, air_step(hla, hlb), 0)
+    lax.fori_loop(0, inner, air_step(hla, hlb), 0, unroll=2)
+    lax.fori_loop(pairs - inner, pairs, air_step(hla, hlb), 0, unroll=2)
+    lax.fori_loop(1, inner + 1, air_step(hlb, hla), 0, unroll=2)
+    lax.fori_loop(pairs - inner - 1, pairs - 1, air_step(hlb, hla), 0, unroll=2)
+    eta_round(2)
+    lax.fori_loop(1, pairs - 1, air_step(hla, hlb), 0, unroll=2)
 
     def air_last(j, carry):
         cols = pl.ds(pl.multiple_of((j - half) * 2 * BLOCK, BLOCK), 2 * BLOCK)
         t_out[:, cols] = air_apply(j, hlb)
         return carry
 
-    lax.fori_loop(half, pairs - half, air_last, 0)
+    lax.fori_loop(half, pairs - half, air_last, 0, unroll=2)
 
     for c in back_sends:
         c.wait_recv()

time: 52.3 us -> 46.2 us (0.88)
  Pallas kernels: 51.6 us -> 45.4 us
    pallas_call x1, Pallas kernels: 46.8 us -> 40.7 us  [body(): pl.pallas_call(functools.partial(main_kernel, n), out_shape=(S((rows_a, n...]
where the time goes in v3:
time: 46.2 us; the launch traced here: 46.1 us
  Pallas kernels  45.4 us (98%)
  between operations  0.64 us (1%)
    pallas_call x1, Pallas kernels, body(): pl.pallas_call(functools.partial(main_kernel, n), out_shape=(S((rows_a, n...  40.7 us
    pallas_call x1, Pallas kernels, body(): pl.pallas_call(last_kernel, out_shape=(S(air.shape, F32), S(mar.shape, F3...  4.76 us

profile of v3, /device:TPU:1, one launch (start us, length us, event | category | flops | bytes accessed | tf_op | source)
XLA Modules:
  0.0 46.1 jit_solution(7725091963669558858)
XLA Ops:
  0.6 40.7 %couple.1 = (f32[224,2048]{1,0:T(8,128)}, f32[256,1024]{1,0:T(8,128)}, f32[4,16,128]{2,1,0:T(8,128)}, f32[8,128]{1,0:T(8,128)}) custom-call(f32[3,72,2048]{2,1,0:T(8,128)} %air.1, f32[1,2048]{1,0:T(1,128)} %bitcast.8, s32[4,2048]{1,0:T(4,128)} %alist_in.1, f32[3,80,1024]{2,1,0:T(8,128)} %mar.1, f32[8,128]{1,0:T(8,128)} %bitcast.10, s32[6,1024]{1,0:T(8,128)} %mlist_in.1, ...), custom_call_target="tpu_custom_call" | custom-call | tf_op jit(solution)/shard_map/couple/pallas_call | solution.py:584
  41.3 4.8 %mix.1 = (f32[3,72,2048]{2,1,0:T(8,128)}, f32[3,80,1024]{2,1,0:T(8,128)}, f32[3,2048]{1,0:T(4,128)}, f32[8,128]{1,0:T(8,128)}) custom-call(f32[224,2048]{1,0:T(8,128)} %get-tuple-element.12.t_in, f32[256,1024]{1,0:T(8,128)} %get-tuple-element.13.y_in, f32[4,16,128]{2,1,0:T(8,128)} %get-tuple-element.14.tot_in, f32[8,128]{1,0:T(8,128)} %get-tuple-element.15.ssh_in, ...), custom_call_target="tpu_custom_call" | custom-call | tf_op jit(solution)/shard_map/mix/pallas_call | solution.py:624
